TPU v7x, 32 devices: a whole 2x2x4 slice. The times are simulated.
32 devices in a mesh: sec: 4 (over x, core), space: 8 (over z, y).
Axes of the slice: x: 2, y: 2, z: 4, core: 2. Of those that a mesh axis runs over, the one named last changes fastest.
Arguments:
- droplet_integrals: float32 [64, 5, 64, 2048], P('sec', None, 'space'), may hold values from -3 to 3, as said below
- flow_number_lengthwise: float32 [64], P('sec'), may hold values from -0.6 to 0.6
- flow_number_crosswise: float32 [64], P('sec'), may hold values from -0.35 to 0.35
- inflow_boundary_integrals: float32 [64, 5], P('sec'), may hold values from 0.2 to 2
- boundary_wall_indicator: int32 [64, 2048], P('space'), may hold values 0 or 1
- inflow_indicator: int32 [64, 2048], P('space'), may hold values 0 or 1
- collision_coefficient: float32 [64, 64], replicated, may hold values from 0.0005 to 0.008
- collision_target_share: float32 [64, 64], replicated, may hold values from 0 to 0.03
- evaporation_speed_stepwise: float32 [64], replicated, may hold values from 0.01 to 0.1
- thermal_factor: float32 [64, 2048], P('space', 'sec'), may hold values from 0.5 to 2
Outputs:
- spray: float32 [64, 5, 64, 2048], P(None, None, 'space', 'sec')
- gas_source: float32 [5, 64, 2048], P(None, 'space', 'sec')
Inputs may be any that keep to these rules, and one draw needn't show every extreme that they name: `droplet_integrals`: moment 0 (mass) is positive, 0.1 or more, in every section and cell.
All inputs are finite; a program needn't handle non-finite values. No bound on the sum of `boundary_wall_indicator` or of `inflow_indicator` on one device may be relied on, other than what follows from the above.
Results may differ from a plain program's by a relative error of at most 0.000084.
Values sent between devices are 32-bit elements; how exact they have to be, the bound alone decides.
No kernel may reach another device: no remote copies, remote signals or barrier semaphores. Data moves between devices by JAX's collectives and lax.ppermute only.
A program may use at most 128 MiB of HBM per device.

v0:
```python
import functools

import jax
import jax.numpy as jnp
from jax import lax
from jax.experimental import pallas as pl
from jax.experimental.pallas import tpu as pltpu
from jax.sharding import PartitionSpec as P

SUB = 4
ROWS = 2 * SUB
LANES = 128
TILE = 8
F32 = jnp.float32
BF16 = jnp.bfloat16
CHAINS = 10
SORT_LIMIT = 44 * 1024 * 1024
SELECT_LIMIT = 50 * 1024 * 1024
VMEM_LIMIT = 8 * 1024 * 1024


def stacked(array):
    *lead, rows, columns = array.shape
    tiles = columns // LANES
    array = array.reshape(*lead, rows, tiles, LANES)
    return jnp.swapaxes(array, -3, -2).reshape(*lead, rows * tiles, LANES)


class Scalars:
    def __init__(self, place_ref, ux_ref, uy_ref, inflow_ref):
        self.me, self.odd = place_ref[0], place_ref[1]
        self.ux_ref, self.uy_ref, self.inflow_ref = ux_ref, uy_ref, inflow_ref

    def ux(self, s):
        return self.ux_ref[s]

    def wind(self, s, blocks):
        return Wind(self.ux_ref[s], self.uy_ref[s], blocks)

    def inflow(self, s, moment):
        return self.inflow_ref[moment, s]


def sublane(shape=(TILE, LANES)):
    return lax.broadcasted_iota(jnp.int32, shape, 0)


class Wind:
    def __init__(self, speed_x, speed_y, blocks):
        self.a, self.b = jnp.abs(speed_x), jnp.abs(speed_y)
        self.own = 1.0 - self.a - self.b
        self.blocks = blocks
        self.positive_x = speed_x > 0.0
        self.positive_y = speed_y > 0.0
        lane = lax.broadcasted_iota(jnp.int32, (TILE, LANES), 1)
        self.lane_shift = jnp.where(self.positive_y, 1, LANES - 1).astype(jnp.int32)
        self.band_shift = jnp.where(self.positive_y, 1, TILE - 1).astype(jnp.int32)
        self.edge = lane == jnp.where(self.positive_y, 0, LANES - 1)
        self.border = sublane() == jnp.where(self.positive_y, 0, TILE - 1)

    def row(self, u, first, last):
        return jnp.where(self.positive_x, first + u, last - u)

    def block(self, j):
        return jnp.where(self.positive_y, j, self.blocks - 1 - j)


def substeps(chains):
    states = [chain[1] for chain in chains]
    for step in range(1, SUB + 1):
        fresh = []
        for (wind, _, code, value), state in zip(chains, states):
            rows = [None] * step
            for u in range(step, ROWS):
                turned = [pltpu.roll(tile, wind.lane_shift, axis=1) for tile in state[u]]
                wrap = pltpu.roll(turned[-1], wind.band_shift, axis=0)
                behind = [jnp.where(wind.border, 0.0, wrap)] + turned[:-1]
                tiles = []
                for j, tile in enumerate(state[u]):
                    side = jnp.where(wind.edge, behind[j], turned[j])
                    moved = wind.own * tile + wind.a * state[u - 1][j] + wind.b * side
                    kind = code(u, j)
                    tiles.append(jnp.where(kind < 0.0, moved, kind * value))
                rows.append(tiles)
            fresh.append(rows)
        states = fresh
    return states


def keep(wind, state, packed):
    blocks = wind.blocks
    for u in range(SUB, ROWS):
        row = wind.row(u, -SUB, ROWS - 1)
        for j, tile in enumerate(state[u]):
            packed[pl.ds(row * blocks + wind.block(j), TILE, stride=SUB * blocks), :] = tile


def scatter(packed, me, outs):
    share = packed.shape[0] // len(outs)
    for k, (out, spot) in enumerate(outs):
        start = pl.multiple_of((me ^ k) * share, share)
        out[spot] = packed[pl.ds(start, share), :]


def select_kernel(outs, blocks, ux_ref, *refs):
    count = sum(outs)
    x_refs, kind_ref, out_refs, code_ref = refs[:count], refs[count], refs[count + 1 : -1], refs[-1]
    per_step, size = x_refs[0].shape[:2]
    step = pl.program_id(0)
    edge = size // 2

    def section(s, carry):
        number = step * per_step + s
        first = jnp.where(ux_ref[number] > 0.0, SUB, 0)
        sources = iter(x_refs)
        for held, out_ref in zip(outs, out_refs):
            for i in range(held):
                x_ref = next(sources)
                for row in range(SUB):
                    for block in range(blocks):
                        spot = i * edge + (row * blocks + block) * TILE
                        source = pl.ds(block * ROWS + first + row, TILE, stride=blocks * ROWS)
                        out_ref[number, spot : spot + TILE, :] = x_ref[s, source, :]
        return carry

    lax.fori_loop(0, per_step, section, 0, unroll=2)

    @pl.when(step == 0)
    def _():
        last = out_refs[0].shape[0] - 2
        for row in range(ROWS):
            for block in range(blocks):
                spot = (row * blocks + block) * TILE
                source = pl.ds(block * ROWS + row, TILE, stride=blocks * ROWS)
                code_ref[spot : spot + TILE, :] = kind_ref[source, :]
        for i in range(2):
            out_refs[0][last + i] = code_ref[i * edge : (i + 1) * edge, :]


def sort_kernel(outs, blocks, ux_ref, x_ref, *refs):
    count = len(refs) - len(outs)
    cell_refs, out_refs = refs[:count], refs[count:]
    per_step = x_ref.shape[0]
    step = pl.program_id(0)
    size = cell_refs[0].shape[1]
    edge = size // 2

    def sort(source, target):
        for band in range(TILE):
            for block in range(blocks):
                tile = source((band * blocks + block) * ROWS)
                target[pl.ds(block * TILE + band, ROWS, stride=blocks * TILE), :] = tile

    def section(s, carry):
        number = step * per_step + s
        first = pl.multiple_of(jnp.where(ux_ref[number] > 0.0, edge, 0), edge)
        for m, cell_ref in enumerate(cell_refs):

            def source(spot, m=m):
                return x_ref[s, m * size + spot : m * size + spot + ROWS, :]

            sort(source, cell_ref.at[number])
        for held, out_ref in zip(outs, out_refs):
            for i, m in enumerate(held):
                out_ref[number, i * edge : (i + 1) * edge, :] = cell_refs[m][
                    number, pl.ds(first, edge), :
                ]
        return carry

    lax.fori_loop(0, per_step, section, 0)


def relay_kernel(total, place_ref, ux_ref, uy_ref, inflow_ref, _, own_ref, far_ref, *out_refs):
    scalars = Scalars(place_ref, ux_ref, uy_ref, inflow_ref)
    size = own_ref.shape[1] // len(out_refs)

    def relay(s, stays):
        def copy(source):
            for i, out_ref in enumerate(out_refs):
                out_ref[s] = source[s, i * size : (i + 1) * size, :]

        pl.when(stays)(lambda: copy(own_ref))
        pl.when(jnp.logical_not(stays))(lambda: copy(far_ref))

    def section(s, carry):
        relay(s, (scalars.ux(s) > 0.0) != (scalars.odd == 1))
        return carry

    lax.fori_loop(0, total, section, 0)
    if own_ref.shape[0] > total:
        relay(total, scalars.odd == 1)
        relay(total + 1, scalars.odd != 1)


def inner_kernel(
    some, blocks, together, place_ref, ux_ref, uy_ref, inflow_ref, _, code_ref, *rest
):
    count = len(some)
    cell_refs, out_refs, packed = rest[:count], rest[count:-1], rest[-1]
    total = cell_refs[0].shape[0]
    scalars = Scalars(place_ref, ux_ref, uy_ref, inflow_ref)
    share = packed.shape[1] // len(out_refs)

    def sections(turn, carry):
        chains, places = [], []
        for i in range(together):
            s = turn * together + i
            wind = scalars.wind(s, blocks)

            def spot(u, j, wind=wind):
                row = wind.row(u, 0, ROWS - 1)
                return pl.ds(pl.multiple_of((row * blocks + wind.block(j)) * TILE, TILE), TILE)

            def code(u, j, spot=spot):
                return code_ref[spot(u, j), :]

            for m, cell_ref in enumerate(cell_refs):
                tiles = [[cell_ref[s, spot(u, j), :] for j in range(blocks)] for u in range(ROWS)]
                chains.append((wind, tiles, code, scalars.inflow(s, some[m])))
                places.append((s, slice(m * share, (m + 1) * share)))
        for c, (chain, state) in enumerate(zip(chains, substeps(chains))):
            keep(chain[0], state, packed.at[c])
        for c, place in enumerate(places):
            scatter(packed.at[c], scalars.me, [(out, place) for out in out_refs])
        return carry

    lax.fori_loop(0, total // together, sections, 0)


def outer_kernel(
    some, halos, starts, blocks, together, place_ref, ux_ref, uy_ref, inflow_ref, _,
    edge_ref, code_ref, *rest
):
    count = len(some)
    cell_refs, rest = rest[:count], rest[count:]
    halo_refs, rest = rest[: sum(halos)], rest[sum(halos) :]
    out_refs, (codes, packed) = rest[:-2], rest[-2:]
    total = cell_refs[0].shape[0]
    scalars = Scalars(place_ref, ux_ref, uy_ref, inflow_ref)
    me, odd = scalars.me, scalars.odd
    edge = SUB * blocks * TILE
    share = packed.shape[1] // len(out_refs)
    last = edge_ref.shape[0] - 2
    codes[:edge] = edge_ref[last + 1]
    codes[edge : 2 * edge] = edge_ref[last]
    codes[2 * edge :] = code_ref[...]

    def sections(turn, carry):
        chains, places = [], []
        for i in range(together):
            s = turn * together + i
            wind = scalars.wind(s, blocks)
            outside = jnp.where(wind.positive_x, 0, edge)
            second = jnp.logical_xor(wind.positive_x, odd == 1)

            def spot(u, j, wind=wind):
                if u < SUB:
                    row = wind.row(u, 0, SUB - 1)
                else:
                    row = wind.row(u, -SUB, ROWS + SUB - 1)
                return (row * blocks + wind.block(j)) * TILE

            def code(u, j, spot=spot, outside=outside):
                at = spot(u, j) + (outside if u < SUB else 2 * edge)
                return codes[pl.ds(pl.multiple_of(at, TILE), TILE), :]

            for m, cell_ref in enumerate(cell_refs):
                held = halo_refs[sum(halos[:m]) : sum(halos[: m + 1])]
                skip = starts[m] * edge
                tiles = []
                for u in range(ROWS):
                    row = []
                    for j in range(blocks):
                        at = spot(u, j) + (skip if u < SUB else 0)
                        at = pl.ds(pl.multiple_of(at, TILE), TILE)
                        if u >= SUB:
                            tile = cell_ref[s, at, :]
                        elif len(held) == 2:
                            tile = jnp.where(second, held[1][s, at, :], held[0][s, at, :])
                        else:
                            tile = held[0][s, at, :]
                        row.append(tile)
                    tiles.append(row)
                chains.append((wind, tiles, code, scalars.inflow(s, some[m])))
                places.append((s, slice(m * share, (m + 1) * share)))
        for c, (chain, state) in enumerate(zip(chains, substeps(chains))):
            keep(chain[0], state, packed.at[c])
        for c, place in enumerate(places):
            scatter(packed.at[c], me, [(out, place) for out in out_refs])
        return carry

    lax.fori_loop(0, total // together, sections, 0)
    if some[0] == 0:
        for s in range(total):
            line = jnp.full((1, LANES), scalars.ux(s), F32)
            for out in out_refs:
                out[total, s : s + 1, :] = line


def split_dot(weights, values):
    high = values.astype(BF16)
    rest = (values - high.astype(F32)).astype(BF16)
    return jnp.dot(
        weights, jnp.concatenate([high, rest, high], axis=0), preferred_element_type=F32
    )


def couple_kernel(first, base, groups, group_size, blocks, *refs):
    me_ref, rate_ref, share_ref, thermal_ref = refs[:4]
    refs = refs[4:]
    sign_refs, inner, outer = refs[:groups], refs[groups : 2 * groups], refs[2 * groups : 3 * groups]
    refs = refs[3 * groups :]
    if first:
        kernel_ref, spray_ref, gas_ref, merge_ref, *scratch = refs
    else:
        merge_ref, _, _, _, spray_ref, gas_ref, *scratch = refs
    rest, total = scratch
    spray_rows = spray_ref.reshape(spray_ref.shape[0] * spray_ref.shape[1], LANES)
    me = me_ref[0]
    moment, step = pl.program_id(0), pl.program_id(1)
    sections = groups * group_size
    size = ROWS * blocks
    half = size // 2
    steps = thermal_ref.shape[0] // size
    inner_spot = pl.ds(pl.multiple_of(((base + moment) * steps + step) * half, half), half)
    outer_spot = pl.ds(pl.multiple_of((moment * steps + step) * half, half), half)
    columns = pl.ds(pl.multiple_of(step * blocks * LANES, LANES), blocks * LANES)
    thermal = [
        thermal_ref[pl.ds(pl.multiple_of(step * size + i * half, half), half), :] for i in range(2)
    ]
    gas = tuple(jnp.zeros((half, LANES), F32) for _ in thermal)
    for k in range(groups):

        def section(s, sums, k=k):
            number = (me ^ k) * group_size + s
            flip = jnp.broadcast_to(sign_refs[k][group_size, pl.ds(s, 1), :], (half, LANES)) > 0.0
            rate = rate_ref[number]
            one, two = inner[k][s, inner_spot, :], outer[k][s, outer_spot, :]
            result = []
            for i, moved in enumerate((jnp.where(flip, two, one), jnp.where(flip, one, two))):
                evaporated = (rate * thermal[i]) * moved
                result.append(sums[i] + evaporated)
                rest[pl.ds(i * half * sections + number, half, stride=sections), :] = moved - evaporated
            return tuple(result)

        gas = lax.fori_loop(0, group_size, section, gas, unroll=4)
    for i in range(2):
        total[i * half : (i + 1) * half, :] = gas[i]
    for block in range(blocks):
        gas_ref[0, :, block * LANES : (block + 1) * LANES] = total[pl.ds(block, ROWS, stride=blocks), :]
    for row in range(ROWS):
        spots = [(row * blocks + block) * sections for block in range(blocks)]
        cells = jnp.concatenate([rest[spot : spot + sections, :] for spot in spots], axis=1)
        if first:
            merge = split_dot(kernel_ref[...], cells)
            merge_ref[row, :, columns] = merge
        else:
            merge = merge_ref[row, :, columns]
        flux = cells * merge
        result = cells - flux + split_dot(share_ref[...], flux)
        for block in range(blocks):
            spray_rows[pl.ds(block * ROWS + row, sections, stride=size), :] = result[
                :, block * LANES : (block + 1) * LANES
            ]


def params(limit=VMEM_LIMIT):
    return pltpu.CompilerParams(vmem_limit_bytes=limit)


def split_weights(weights):
    high = lax.reduce_precision(weights, 8, 7)
    return jnp.concatenate([high, high, weights - high], axis=1).astype(BF16)


def shards(
    droplet_integrals,
    flow_number_lengthwise,
    flow_number_crosswise,
    inflow_boundary_integrals,
    boundary_wall_indicator,
    inflow_indicator,
    collision_coefficient,
    collision_target_share,
    evaporation_speed_stepwise,
    thermal_factor,
):
    x, ux, uy = droplet_integrals, flow_number_lengthwise, flow_number_crosswise
    group_size, moments, rows, columns = x.shape
    groups = lax.axis_size("sec")
    slabs = lax.axis_size("space")
    sections = groups * group_size
    width = columns // groups
    blocks = columns // (TILE * LANES)
    size = columns // LANES * ROWS
    share_size = size // 2 // groups
    assert rows == ROWS and slabs % 2 == 0 and TILE % groups == 0

    swap = [(i, i ^ 1) for i in range(slabs)]
    outward = [(i, i + 2) for i in range(0, slabs - 2, 2)] + [(i, i - 2) for i in range(3, slabs, 2)]
    inward = [(j, i) for i, j in outward]

    smem = pl.BlockSpec(memory_space=pltpu.SMEM)
    anywhere = pl.BlockSpec(memory_space=pl.ANY)
    cells = stacked(x).reshape(group_size, moments * size, LANES)

    vmem = pl.BlockSpec(memory_space=pltpu.VMEM)
    edge = SUB * blocks * TILE
    place = jnp.stack([lax.axis_index("sec"), lax.axis_index("space") % 2]).astype(jnp.int32)

    def send(parts, first, last, *events):
        return [
            lax.ppermute(after(parts[k], *events), "sec", [(i, i ^ k) for i in range(groups)])
            for k in range(first, last)
        ]

    def after(value, *events):
        return lax.optimization_barrier((value, *events))[0]

    def select(outs):
        some = sum(outs, ())
        per_step = group_size // 2
        shapes = [
            (group_size + 2 * (i == 0), len(held) * edge, LANES) for i, held in enumerate(outs)
        ] + [(size, LANES)]
        kind = jnp.where(inflow_indicator > 0, 1.0, -1.0)
        kind = jnp.where(boundary_wall_indicator > 0, 0.0, kind).astype(F32)
        return pl.pallas_call(
            functools.partial(select_kernel, tuple(len(held) for held in outs), blocks),
            grid=(group_size // per_step,),
            in_specs=[smem]
            + [
                pl.BlockSpec((per_step, size, LANES), lambda g, moment=moment: (g, moment, 0))
                for moment in some
            ]
            + [vmem],
            out_specs=[vmem] * len(shapes),
            out_shape=[jax.ShapeDtypeStruct(shape, F32) for shape in shapes],
            compiler_params=params(SELECT_LIMIT),
            cost_estimate=cost(len(some), x.size),
            name="select_upwind_rows",
        )(after(ux, place), *[cells] * len(some), stacked(kind))

    def sort(outs, last):
        per_step = group_size // 4
        shapes = [(group_size, size, LANES)] * moments
        shapes += [(group_size, len(held) * edge, LANES) for held in outs]
        made = pl.pallas_call(
            functools.partial(sort_kernel, outs, blocks),
            grid=(group_size // per_step,),
            in_specs=[
                smem, pl.BlockSpec((per_step, moments * size, LANES), lambda g: (g, 0, 0))
            ],
            out_specs=[vmem] * len(shapes),
            out_shape=[jax.ShapeDtypeStruct(shape, F32) for shape in shapes],
            compiler_params=params(SORT_LIMIT),
            cost_estimate=cost(moments, x.size),
            name="sort_cells",
        )(after(ux, last), cells)
        return made[:moments], made[moments:]

    def cost(count, amount):
        return pl.CostEstimate(
            flops=amount * count, bytes_accessed=amount * count, transcendentals=0
        )

    def whole(kernel, name, last, operands, out_shapes, scratch=(), count=1):
        return pl.pallas_call(
            kernel,
            in_specs=[smem] * 4 + [anywhere] + [vmem] * len(operands),
            out_specs=[vmem] * len(out_shapes),
            out_shape=[jax.ShapeDtypeStruct(shape, F32) for shape in out_shapes],
            scratch_shapes=list(scratch),
            compiler_params=params(),
            cost_estimate=cost(count, x.size),
            name=name,
        )(place, ux, uy, inflow_boundary_integrals.T, last, *operands)

    def together(some):
        count = 1
        while 2 * count * len(some) <= CHAINS and group_size % (2 * count) == 0:
            count *= 2
        return count

    def transport_inner(some, last):
        return whole(
            functools.partial(inner_kernel, some, blocks, together(some)),
            "transport_inner_rows",
            last,
            [code, *[own[moment] for moment in some]],
            [(group_size, len(some) * share_size, LANES)] * groups,
            [pltpu.VMEM((together(some) * len(some), size // 2, LANES), F32)],
            count=len(some),
        )

    def transport_outer(some, halos, last, starts=None):
        return whole(
            functools.partial(
                outer_kernel,
                some,
                tuple(len(h) for h in halos),
                starts or (0,) * len(some),
                blocks,
                together(some),
            ),
            "transport_outer_rows",
            last,
            [near_0, code, *[own[moment] for moment in some], *sum(halos, ())],
            [(group_size + (some[0] == 0), len(some) * share_size, LANES)] * groups,
            [
                pltpu.VMEM((2 * edge + size, LANES), F32),
                pltpu.VMEM((together(some) * len(some), size // 2, LANES), F32),
            ],
            count=len(some),
        )

    def relay(own, far, count, last):
        return whole(
            functools.partial(relay_kernel, group_size),
            "relay_upwind_rows",
            last,
            [own, far],
            [(own.shape[0], own.shape[1] // count, LANES)] * count,
        )

    def swapped(array):
        return lax.ppermute(array, "space", swap)

    def hopped(array, pairs):
        return lax.ppermute(array, "space", pairs)

    share = split_weights(collision_target_share)
    kernel = split_weights(collision_coefficient)
    step_width = blocks * LANES
    steps = width // step_width
    step_size = ROWS * blocks
    thermal = thermal_factor.reshape(ROWS, steps, blocks, LANES).swapaxes(0, 1)
    thermal = thermal.reshape(steps * step_size, LANES)
    spray_type = jax.ShapeDtypeStruct((sections, moments * steps * step_size, LANES), F32)
    gas_type = jax.ShapeDtypeStruct((moments, rows, width), F32)
    merge_type = jax.ShapeDtypeStruct((rows, sections, width), F32)
    made = {}

    def couple(some, inner, base, outer, last):
        first = some[0] == 0

        in_specs = [smem] * 2 + [vmem] * (2 + 3 * groups)
        operands = [place, evaporation_speed_stepwise, share, thermal]
        operands += list(made.setdefault("sign", outer)) + list(inner) + list(outer)
        out_specs = [
            pl.BlockSpec(
                (sections, step_size, LANES), lambda m, j: (0, (some[0] + m) * steps + j, 0)
            ),
            pl.BlockSpec((1, rows, step_width), lambda m, j: (some[0] + m, 0, j)),
        ]
        out_shape = [spray_type, gas_type]
        aliases = {}
        if first:
            in_specs.append(vmem)
            operands.append(kernel)
            out_specs.append(vmem)
            out_shape.append(merge_type)
        else:
            aliases = {len(operands) + 1: 0, len(operands) + 2: 1}
            in_specs += [vmem, anywhere, anywhere, anywhere]
            operands += [made["merge"], made["spray"], made["gas"], last]
        result = pl.pallas_call(
            functools.partial(couple_kernel, first, base, groups, group_size, blocks),
            grid=(len(some), steps),
            in_specs=in_specs,
            out_specs=out_specs,
            out_shape=out_shape,
            input_output_aliases=aliases,
            scratch_shapes=[
                pltpu.VMEM((sections * step_size, LANES), F32),
                pltpu.VMEM((step_size, LANES), F32),
            ],
            compiler_params=params(),
            cost_estimate=pl.CostEstimate(
                flops=sections * rows * width * sections * 2 * len(some),
                bytes_accessed=sections * rows * width * 12 * len(some),
                transcendentals=0,
            ),
            name="couple_sections",
        )(*operands)
        made.update(zip(("spray", "gas", "merge"), result))

    chosen_0, chosen_12, code = select(((0,), (1, 2)))
    near_12 = swapped(chosen_12)
    far_0 = hopped(chosen_0, inward)
    own, (chosen_34,) = sort(((3, 4),), code)
    far_34 = hopped(chosen_34, inward)
    inner = transport_inner(tuple(range(moments)), chosen_34)
    far_in = send(inner, 2, groups)
    (relayed_0,) = relay(chosen_0, far_0, 1, inner[0])
    near_0 = swapped(relayed_0)
    far_12 = hopped(after(near_12, relayed_0), outward)
    (relayed_34,) = relay(chosen_34, far_34, 1, after(relayed_0, near_0))
    near_34 = swapped(relayed_34)
    outer_0 = transport_outer((0,), ((near_0,),), after(relayed_34, *far_in))
    far_of_0 = send(outer_0, 2, groups, *far_in)
    pair_in = send(inner, 1, 2, outer_0[0])
    pair_of_0 = send(outer_0, 1, 2, far_12, *pair_in)
    outer_12 = transport_outer(
        (1, 2), ((near_12, far_12), (near_12, far_12)), outer_0[0], (0, 1)
    )
    far_of_12 = send(outer_12, 2, groups, near_34)
    outer_3 = transport_outer((3,), ((near_34,),), after(outer_12[0], *far_of_0), (0,))
    far_of_3 = send(outer_3, 2, groups)
    pair_of_12 = send(outer_12, 1, 2, *pair_of_0)
    sent = [inner[0], *pair_in, *far_in]
    couple((0,), sent, 0, [outer_0[0], *pair_of_0, *far_of_0], outer_3[0])
    outer_4 = transport_outer((4,), ((near_34,),), made["merge"], (1,))
    pair_of_3 = send(outer_3, 1, 2, *pair_of_12)
    sent_4 = [outer_4[0]] + send(outer_4, 1, groups)
    couple((1, 2), sent, 1, [outer_12[0], *pair_of_12, *far_of_12], outer_4[0])
    couple((3,), sent, 3, [outer_3[0], *pair_of_3, *far_of_3], outer_4[0])
    couple((4,), sent, 4, sent_4, outer_4[0])
    spray = jnp.swapaxes(
        made["spray"].reshape(sections, moments, width // LANES, rows, LANES), 2, 3
    )
    return spray.reshape(sections, moments, rows, width), made["gas"]


def solution(mesh):
    return jax.shard_map(
        shards,
        mesh=mesh,
        in_specs=(
            P("sec", None, "space", None),
            P("sec"),
            P("sec"),
            P("sec", None),
            P("space", None),
            P("space", None),
            P(),
            P(),
            P(),
            P("space", "sec"),
        ),
        out_specs=(P(None, None, "space", "sec"), P(None, "space", "sec")),
        check_vma=False,
    )
```

profile of v0, /device:TPU:0, one launch (start us, length us, event | category | flops | bytes accessed | tf_op | source)
XLA Modules:
  0.0 101.9 jit_solution(14308083082298297580)
XLA Ops:
  0.6 0.1 pad_add_fusion.place_ref.refs_0_
  0.7 0.9 select_bitcast_fusion.refs_3_
  1.6 0.6 copy-done.1
  2.3 2.2 %select_upwind_rows.1 = (f32[18,64,128]{2,1,0:T(8,128)S(1)}, f32[16,128,128]{2,1,0:T(8,128)S(1)}, f32[128,128]{1,0:T(8,128)S(1)}) custom-call(f32[16]{0:T(128)S(1)} %copy-done.1, f32[16,640,128]{2,1,0:T(8,128)} %bitcast.34, f32[16,640,128]{2,1,0:T(8,128)} %bitcast.35, f32[16,640,128]{2,1,0:T(8,128)} %bitcast.36, f32[128,128]{1,0:T(8,128)S(1)} %select_bitcast_fusion.refs_3_), custom_call_target="tpu_custom_call" | custom-call | flops 3932160 | bytes 3932160 | tf_op jit(solution)/shard_map/select_upwind_rows/pallas_call | solution.py:428
  4.4 0.0 copy-start
  4.5 3.0 %collective-permute-start.5 = (f32[16,128,128]{2,1,0:T(8,128)S(1)}, f32[16,128,128]{2,1,0:T(8,128)S(1)}, u32[]{:S(2)}, u32[]{:S(2)}) collective-permute-start(f32[16,128,128]{2,1,0:T(8,128)S(1)} %get-tuple-element.71), channel_id=1, source_target_pairs={{0,1},{1,0},{2,3},{3,2},{4,5},{5,4},{6,7},{7,6},{8,9},{9,8},{10,11... | collective-permute-start | bytes 3145736 | tf_op jit(solution)/shard_map/ppermute | solution.py:527
  7.5 1.3 %collective-permute-start = (f32[18,64,128]{2,1,0:T(8,128)S(1)}, f32[18,64,128]{2,1,0:T(8,128)S(1)}, u32[]{:S(2)}, u32[]{:S(2)}) collective-permute-start(f32[18,64,128]{2,1,0:T(8,128)S(1)} %get-tuple-element.64.own_ref), channel_id=1, source_target_pairs={{2,0},{4,2},{6,4},{1,3},{3,5},{5,7},{10,8},{12,10},{14,12},{9,11},... | collective-permute-start | bytes 1769480 | tf_op jit(solution)/shard_map/ppermute | solution.py:530
  8.8 4.0 %sort_cells.1 = (f32[16,128,128]{2,1,0:T(8,128)S(1)}, f32[16,128,128]{2,1,0:T(8,128)S(1)}, f32[16,128,128]{2,1,0:T(8,128)S(1)}, f32[16,128,128]{2,1,0:T(8,128)S(...) custom-call(f32[16]{0:T(128)S(1)} %copy-done.2, f32[16,640,128]{2,1,0:T(8,128)} %bitcast.37), custom_call_target="tpu_custom_call" | custom-call | flops 6553600 | bytes 6553600 | tf_op jit(solution)/shard_map/sort_cells/pallas_call | solution.py:448
  12.8 1.3 %collective-permute-start.2 = (f32[16,128,128]{2,1,0:T(8,128)S(1)}, f32[16,128,128]{2,1,0:T(8,128)S(1)}, u32[]{:S(2)}, u32[]{:S(2)}) collective-permute-start(f32[16,128,128]{2,1,0:T(8,128)S(1)} %get-tuple-element.57._.own_ref), channel_id=1, source_target_pairs={{2,0},{4,2},{6,4},{1,3},{3,5},{5,7},{10,8},{12,10},{14,12},{9,11},... | collective-permute-start | bytes 3145736 | tf_op jit(solution)/shard_map/ppermute | solution.py:530
  14.1 6.3 %transport_inner_rows.1 = (f32[16,80,128]{2,1,0:T(8,128)S(1)}, f32[16,80,128]{2,1,0:T(8,128)S(1)}, f32[16,80,128]{2,1,0:T(8,128)S(1)}, f32[16,80,128]{2,1,0:T(8,128)S(1)}) custom-call(s32[2]{0:T(128)S(1)} %pad_add_fusion.place_ref.refs_0_, f32[16]{0:T(128)S(1)} %copy-done.2, f32[16]{0:T(128)S(1)} %copy-done.3, f32[5,16]{1,0:T(8,128)S(1)} %bitcast.27, ...), custom_call_target="tpu_custom_call" | custom-call | flops 6553600 | bytes 6553600 | tf_op jit(solution)/shard_map/transport_inner_rows/pallas_call | solution.py:468
  20.4 0.0 copy-start.5
  20.5 5.2 %collective-permute-done.far_ref = f32[18,64,128]{2,1,0:T(8,128)S(1)} collective-permute-done((f32[18,64,128]{2,1,0:T(8,128)S(1)}, f32[18,64,128]{2,1,0:T(8,128)S(1)}, u32[]{:S(2)}, u32[]{:S(2)}) %collective-permute-start) | collective-permute-done | bytes 589856 | tf_op jit(solution)/shard_map/ppermute | solution.py:530
  25.6 0.9 relay_upwind_rows.2._
  26.6 0.1 collective-permute-start.1
  26.7 0.1 collective-permute-start.4
  26.7 1.6 %collective-permute-start.3 = (f32[16,80,128]{2,1,0:T(8,128)S(1)}, f32[16,80,128]{2,1,0:T(8,128)S(1)}, u32[]{:S(2)}, u32[]{:S(2)}) collective-permute-start(f32[16,80,128]{2,1,0:T(8,128)S(1)} %get-tuple-element.66), channel_id=1, source_target_pairs={{0,16},{8,24},{16,0},{24,8},{1,17},{9,25},{17,1},{25,9},{2,18},{10... | collective-permute-start | bytes 1966088 | tf_op jit(solution)/shard_map/ppermute | solution.py:413
  28.3 3.2 %collective-permute-done.5.rest_2_.rest_4_ = f32[16,128,128]{2,1,0:T(8,128)S(1)} collective-permute-done((f32[16,128,128]{2,1,0:T(8,128)S(1)}, f32[16,128,128]{2,1,0:T(8,128)S(1)}, u32[]{:S(2)}, u32[]{:S(2)}) %collective-permute-start.5) | collective-permute-done | bytes 1048608 | tf_op jit(solution)/shard_map/ppermute | solution.py:527
  31.5 4.1 %collective-permute-start.6 = (f32[16,128,128]{2,1,0:T(8,128)S(1)}, f32[16,128,128]{2,1,0:T(8,128)S(1)}, u32[]{:S(2)}, u32[]{:S(2)}) collective-permute-start(f32[16,128,128]{2,1,0:T(8,128)S(1)} %collective-permute-done.5.rest_2_.rest_4_), channel_id=1, source_target_pairs={{0,2},{2,4},{4,6},{3,1},{5,3},{7,5},{8,10},{10,12},{12,14},{11,9},... | collective-permute-start | bytes 3145736 | tf_op jit(solution)/shard_map/ppermute | solution.py:530
  35.6 7.7 %collective-permute-done.1.edge_ref.rest_1_ = f32[18,64,128]{2,1,0:T(8,128)S(1)} collective-permute-done((f32[18,64,128]{2,1,0:T(8,128)S(1)}, f32[18,64,128]{2,1,0:T(8,128)S(1)}, u32[]{:S(2)}, u32[]{:S(2)}) %collective-permute-start.1) | collective-permute-done | bytes 589856 | tf_op jit(solution)/shard_map/ppermute | solution.py:527
  43.3 3.3 %collective-permute-done.2.far_ref = f32[16,128,128]{2,1,0:T(8,128)S(1)} collective-permute-done((f32[16,128,128]{2,1,0:T(8,128)S(1)}, f32[16,128,128]{2,1,0:T(8,128)S(1)}, u32[]{:S(2)}, u32[]{:S(2)}) %collective-permute-start.2) | collective-permute-done | bytes 1048608 | tf_op jit(solution)/shard_map/ppermute | solution.py:530
  46.6 1.0 relay_upwind_rows.3._
  47.6 0.1 collective-permute-start.11
  47.7 10.1 %collective-permute-done.3.refs_10_ = f32[16,80,128]{2,1,0:T(8,128)S(1)} collective-permute-done((f32[16,80,128]{2,1,0:T(8,128)S(1)}, f32[16,80,128]{2,1,0:T(8,128)S(1)}, u32[]{:S(2)}, u32[]{:S(2)}) %collective-permute-start.3) | collective-permute-done | bytes 655392 | tf_op jit(solution)/shard_map/ppermute | solution.py:413
  57.8 2.3 %transport_outer_rows.4 = (f32[17,16,128]{2,1,0:T(8,128)S(1)}, f32[17,16,128]{2,1,0:T(8,128)S(1)}, f32[17,16,128]{2,1,0:T(8,128)S(1)}, f32[17,16,128]{2,1,0:T(8,128)S(1)}) custom-call(s32[2]{0:T(128)S(1)} %pad_add_fusion.place_ref.refs_0_, f32[16]{0:T(128)S(1)} %copy-done.2, f32[16]{0:T(128)S(1)} %copy-done.3, f32[5,16]{1,0:T(8,128)S(1)} %bitcast.30, ...), custom_call_target="tpu_custom_call" | custom-call | flops 1310720 | bytes 1310720 | tf_op jit(solution)/shard_map/transport_outer_rows/pallas_call | solution.py:468
  60.1 0.0 copy-start.7
  60.1 0.1 collective-permute-start.7
  60.3 2.0 %collective-permute-done.7.refs_9_ = f32[16,80,128]{2,1,0:T(8,128)S(1)} collective-permute-done((f32[16,80,128]{2,1,0:T(8,128)S(1)}, f32[16,80,128]{2,1,0:T(8,128)S(1)}, u32[]{:S(2)}, u32[]{:S(2)}) %collective-permute-start.7) | collective-permute-done | bytes 655392 | tf_op jit(solution)/shard_map/ppermute | solution.py:413
  62.3 0.1 collective-permute-start.8
  62.5 0.4 collective-permute-start.10
  62.8 1.7 %collective-permute-start.9 = (f32[17,16,128]{2,1,0:T(8,128)S(1)}, f32[17,16,128]{2,1,0:T(8,128)S(1)}, u32[]{:S(2)}, u32[]{:S(2)}) collective-permute-start(f32[17,16,128]{2,1,0:T(8,128)S(1)} %get-tuple-element.77), channel_id=1, source_target_pairs={{0,16},{8,24},{16,0},{24,8},{1,17},{9,25},{17,1},{25,9},{2,18},{10... | collective-permute-start | bytes 417800 | tf_op jit(solution)/shard_map/ppermute | solution.py:413
  64.5 3.4 %transport_outer_rows.6 = (f32[16,32,128]{2,1,0:T(8,128)S(1)}, f32[16,32,128]{2,1,0:T(8,128)S(1)}, f32[16,32,128]{2,1,0:T(8,128)S(1)}, f32[16,32,128]{2,1,0:T(8,128)S(1)}) custom-call(s32[2]{0:T(128)S(1)} %pad_add_fusion.place_ref.refs_0_, f32[16]{0:T(128)S(1)} %copy-done.2, f32[16]{0:T(128)S(1)} %copy-done.3, f32[5,16]{1,0:T(8,128)S(1)} %bitcast.31, ...), custom_call_target="tpu_custom_call" | custom-call | flops 2621440 | bytes 2621440 | tf_op jit(solution)/shard_map/transport_outer_rows/pallas_call | solution.py:468
  68.0 3.4 %collective-permute-done.11.rest_1_ = f32[16,128,128]{2,1,0:T(8,128)S(1)} collective-permute-done((f32[16,128,128]{2,1,0:T(8,128)S(1)}, f32[16,128,128]{2,1,0:T(8,128)S(1)}, u32[]{:S(2)}, u32[]{:S(2)}) %collective-permute-start.11) | collective-permute-done | bytes 1048608 | tf_op jit(solution)/shard_map/ppermute | solution.py:527
  71.4 1.5 %collective-permute-start.19 = (f32[16,32,128]{2,1,0:T(8,128)S(1)}, f32[16,32,128]{2,1,0:T(8,128)S(1)}, u32[]{:S(2)}, u32[]{:S(2)}) collective-permute-start(f32[16,32,128]{2,1,0:T(8,128)S(1)} %get-tuple-element.95), channel_id=1, source_target_pairs={{0,16},{8,24},{16,0},{24,8},{1,17},{9,25},{17,1},{25,9},{2,18},{10... | collective-permute-start | bytes 786440 | tf_op jit(solution)/shard_map/ppermute | solution.py:413
  72.9 0.3 collective-permute-start.15
  73.3 2.3 %transport_outer_rows.7 = (f32[16,16,128]{2,1,0:T(8,128)S(1)}, f32[16,16,128]{2,1,0:T(8,128)S(1)}, f32[16,16,128]{2,1,0:T(8,128)S(1)}, f32[16,16,128]{2,1,0:T(8,128)S(1)}) custom-call(s32[2]{0:T(128)S(1)} %pad_add_fusion.place_ref.refs_0_, f32[16]{0:T(128)S(1)} %copy-done.2, f32[16]{0:T(128)S(1)} %copy-done.3, f32[5,16]{1,0:T(8,128)S(1)} %bitcast.32, ...), custom_call_target="tpu_custom_call" | custom-call | flops 1310720 | bytes 1310720 | tf_op jit(solution)/shard_map/transport_outer_rows/pallas_call | solution.py:468
  75.6 1.6 %collective-permute-start.17 = (f32[16,16,128]{2,1,0:T(8,128)S(1)}, f32[16,16,128]{2,1,0:T(8,128)S(1)}, u32[]{:S(2)}, u32[]{:S(2)}) collective-permute-start(f32[16,16,128]{2,1,0:T(8,128)S(1)} %get-tuple-element.92), channel_id=1, source_target_pairs={{0,16},{8,24},{16,0},{24,8},{1,17},{9,25},{17,1},{25,9},{2,18},{10... | collective-permute-start | bytes 393224 | tf_op jit(solution)/shard_map/ppermute | solution.py:413
  77.1 0.1 pad_maximum_fusion.1.refs_16_
  77.2 0.1 pad_maximum_fusion.refs_2_
  77.3 0.1 collective-permute-start.18
  77.4 0.6 collective-permute-start.16
  78.1 3.6 %couple_sections.4 = (f32[64,160,128]{2,1,0:T(8,128)}, f32[5,8,512]{2,1,0:T(8,128)}, f32[8,64,512]{2,1,0:T(8,128)S(1)}) custom-call(s32[2]{0:T(128)S(1)} %pad_add_fusion.place_ref.refs_0_, f32[64]{0:T(128)S(1)} %copy-done.4, bf16[64,192]{1,0:T(8,128)(2,1)S(1)} %pad_maximum_fusion.refs_2_, f32[32,128]{1,0:T(8,128)S(1)} %bitcast.23, ...), custom_call_target="tpu_custom_call" | custom-call | flops 33554432 | bytes 3145728 | tf_op jit(solution)/shard_map/couple_sections/pallas_call | solution.py:567
  81.6 2.3 %transport_outer_rows.5 = (f32[16,16,128]{2,1,0:T(8,128)S(1)}, f32[16,16,128]{2,1,0:T(8,128)S(1)}, f32[16,16,128]{2,1,0:T(8,128)S(1)}, f32[16,16,128]{2,1,0:T(8,128)S(1)}) custom-call(s32[2]{0:T(128)S(1)} %pad_add_fusion.place_ref.refs_0_, f32[16]{0:T(128)S(1)} %copy-done.2, f32[16]{0:T(128)S(1)} %copy-done.3, f32[5,16]{1,0:T(8,128)S(1)} %bitcast.33, ...), custom_call_target="tpu_custom_call" | custom-call | flops 1310720 | bytes 1310720 | tf_op jit(solution)/shard_map/transport_outer_rows/pallas_call | solution.py:468
  83.9 4.6 %collective-permute-done.17.refs_14_ = f32[16,16,128]{2,1,0:T(8,128)S(1)} collective-permute-done((f32[16,16,128]{2,1,0:T(8,128)S(1)}, f32[16,16,128]{2,1,0:T(8,128)S(1)}, u32[]{:S(2)}, u32[]{:S(2)}) %collective-permute-start.17) | collective-permute-done | bytes 131104 | tf_op jit(solution)/shard_map/ppermute | solution.py:413
  88.5 1.0 collective-permute-start.12
  89.4 1.2 %collective-permute-start.14 = (f32[16,16,128]{2,1,0:T(8,128)S(1)}, f32[16,16,128]{2,1,0:T(8,128)S(1)}, u32[]{:S(2)}, u32[]{:S(2)}) collective-permute-start(f32[16,16,128]{2,1,0:T(8,128)S(1)} %get-tuple-element.84), channel_id=1, source_target_pairs={{0,24},{8,16},{16,8},{24,0},{1,25},{9,17},{17,9},{25,1},{2,26},{10... | collective-permute-start | bytes 393224 | tf_op jit(solution)/shard_map/ppermute | solution.py:413
  90.6 4.9 %couple_sections.5 = (f32[64,160,128]{2,1,0:T(8,128)}, f32[5,8,512]{2,1,0:T(8,128)}) custom-call(s32[2]{0:T(128)S(1)} %pad_add_fusion.place_ref.refs_0_, f32[64]{0:T(128)S(1)} %copy-done.4, bf16[64,192]{1,0:T(8,128)(2,1)S(1)} %pad_maximum_fusion.refs_2_, f32[32,128]{1,0:T(8,128)S(1)} %bitcast.24, ...), custom_call_target="tpu_custom_call", output_to_operand_aliasing={{0}: (17, {}), {1}: (18, {})} | custom-call | flops 67108864 | bytes 6291456 | tf_op jit(solution)/shard_map/couple_sections/pallas_call | solution.py:567
  95.5 3.2 %couple_sections.6 = (f32[64,160,128]{2,1,0:T(8,128)}, f32[5,8,512]{2,1,0:T(8,128)}) custom-call(s32[2]{0:T(128)S(1)} %pad_add_fusion.place_ref.refs_0_, f32[64]{0:T(128)S(1)} %copy-done.4, bf16[64,192]{1,0:T(8,128)(2,1)S(1)} %pad_maximum_fusion.refs_2_, f32[32,128]{1,0:T(8,128)S(1)} %bitcast.25, ...), custom_call_target="tpu_custom_call", output_to_operand_aliasing={{0}: (17, {}), {1}: (18, {})} | custom-call | flops 33554432 | bytes 3145728 | tf_op jit(solution)/shard_map/couple_sections/pallas_call | solution.py:567
  98.7 3.2 %couple_sections.7 = (f32[64,160,128]{2,1,0:T(8,128)}, f32[5,8,512]{2,1,0:T(8,128)}) custom-call(s32[2]{0:T(128)S(1)} %pad_add_fusion.place_ref.refs_0_, f32[64]{0:T(128)S(1)} %copy-done.4, bf16[64,192]{1,0:T(8,128)(2,1)S(1)} %pad_maximum_fusion.refs_2_, f32[32,128]{1,0:T(8,128)S(1)} %bitcast.26, ...), custom_call_target="tpu_custom_call", output_to_operand_aliasing={{0}: (17, {}), {1}: (18, {})} | custom-call | flops 33554432 | bytes 3145728 | tf_op jit(solution)/shard_map/couple_sections/pallas_call | solution.py:567
  (30 shorter events, 0.1 us)
Async XLA Ops:
  1.6 0.7 copy-start.1
  2.3 6.5 %copy-start.2 = (f32[16]{0:T(128)S(1)}, f32[16]{0:T(128)}, u32[]{:S(2)}) copy-start(f32[16]{0:T(128)} %ux_ref.15) | copy-start | bytes 196
  4.4 9.7 %copy-start = (f32[16,5]{0,1:T(8,128)S(1)}, f32[16,5]{0,1:T(8,128)}, u32[]{:S(2)}) copy-start(f32[16,5]{0,1:T(8,128)} %param.13) | copy-start | bytes 964
  4.5 9.7 %copy-start.3 = (f32[16]{0:T(128)S(1)}, f32[16]{0:T(128)}, u32[]{:S(2)}) copy-start(f32[16]{0:T(128)} %uy_ref.13) | copy-start | bytes 196
  4.5 27.0 %collective-permute-start.5 = (f32[16,128,128]{2,1,0:T(8,128)S(1)}, f32[16,128,128]{2,1,0:T(8,128)S(1)}, u32[]{:S(2)}, u32[]{:S(2)}) collective-permute-start(f32[16,128,128]{2,1,0:T(8,128)S(1)} %get-tuple-element.71), channel_id=1, source_target_pairs={{0,1},{1,0},{2,3},{3,2},{4,5},{5,4},{6,7},{7,6},{8,9},{9,8},{10,11... | collective-permute-start | bytes 3145736 | tf_op jit(solution)/shard_map/ppermute | solution.py:527
  7.5 18.1 %collective-permute-start = (f32[18,64,128]{2,1,0:T(8,128)S(1)}, f32[18,64,128]{2,1,0:T(8,128)S(1)}, u32[]{:S(2)}, u32[]{:S(2)}) collective-permute-start(f32[18,64,128]{2,1,0:T(8,128)S(1)} %get-tuple-element.64.own_ref), channel_id=1, source_target_pairs={{2,0},{4,2},{6,4},{1,3},{3,5},{5,7},{10,8},{12,10},{14,12},{9,11},... | collective-permute-start | bytes 1769480 | tf_op jit(solution)/shard_map/ppermute | solution.py:530
  12.8 33.8 %collective-permute-start.2 = (f32[16,128,128]{2,1,0:T(8,128)S(1)}, f32[16,128,128]{2,1,0:T(8,128)S(1)}, u32[]{:S(2)}, u32[]{:S(2)}) collective-permute-start(f32[16,128,128]{2,1,0:T(8,128)S(1)} %get-tuple-element.57._.own_ref), channel_id=1, source_target_pairs={{2,0},{4,2},{6,4},{1,3},{3,5},{5,7},{10,8},{12,10},{14,12},{9,11},... | collective-permute-start | bytes 3145736 | tf_op jit(solution)/shard_map/ppermute | solution.py:530
  20.4 42.0 %copy-start.5 = (f32[64,64]{1,0:T(8,128)S(1)}, f32[64,64]{1,0:T(8,128)}, u32[]{:S(2)}) copy-start(f32[64,64]{1,0:T(8,128)} %param.16) | copy-start | bytes 49156
  26.6 16.7 %collective-permute-start.1 = (f32[18,64,128]{2,1,0:T(8,128)S(1)}, f32[18,64,128]{2,1,0:T(8,128)S(1)}, u32[]{:S(2)}, u32[]{:S(2)}) collective-permute-start(f32[18,64,128]{2,1,0:T(8,128)S(1)} %relay_upwind_rows.2._), channel_id=1, source_target_pairs={{0,1},{1,0},{2,3},{3,2},{4,5},{5,4},{6,7},{7,6},{8,9},{9,8},{10,11... | collective-permute-start | bytes 1769480 | tf_op jit(solution)/shard_map/ppermute | solution.py:527
  26.7 21.0 %collective-permute-start.4 = (f32[16,80,128]{2,1,0:T(8,128)S(1)}, f32[16,80,128]{2,1,0:T(8,128)S(1)}, u32[]{:S(2)}, u32[]{:S(2)}) collective-permute-start(f32[16,80,128]{2,1,0:T(8,128)S(1)} %get-tuple-element.67), channel_id=1, source_target_pairs={{0,24},{8,16},{16,8},{24,0},{1,25},{9,17},{17,9},{25,1},{2,26},{10... | collective-permute-start | bytes 1966088 | tf_op jit(solution)/shard_map/ppermute | solution.py:413
  26.7 31.1 %collective-permute-start.3 = (f32[16,80,128]{2,1,0:T(8,128)S(1)}, f32[16,80,128]{2,1,0:T(8,128)S(1)}, u32[]{:S(2)}, u32[]{:S(2)}) collective-permute-start(f32[16,80,128]{2,1,0:T(8,128)S(1)} %get-tuple-element.66), channel_id=1, source_target_pairs={{0,16},{8,24},{16,0},{24,8},{1,17},{9,25},{17,1},{25,9},{2,18},{10... | collective-permute-start | bytes 1966088 | tf_op jit(solution)/shard_map/ppermute | solution.py:413
  31.5 30.8 %collective-permute-start.6 = (f32[16,128,128]{2,1,0:T(8,128)S(1)}, f32[16,128,128]{2,1,0:T(8,128)S(1)}, u32[]{:S(2)}, u32[]{:S(2)}) collective-permute-start(f32[16,128,128]{2,1,0:T(8,128)S(1)} %collective-permute-done.5.rest_2_.rest_4_), channel_id=1, source_target_pairs={{0,2},{2,4},{4,6},{3,1},{5,3},{7,5},{8,10},{10,12},{12,14},{11,9},... | collective-permute-start | bytes 3145736 | tf_op jit(solution)/shard_map/ppermute | solution.py:530
  47.6 25.7 %copy-start.6 = (f32[64,64]{1,0:T(8,128)S(1)}, f32[64,64]{1,0:T(8,128)}, u32[]{:S(2)}) copy-start(f32[64,64]{1,0:T(8,128)} %param.17) | copy-start | bytes 49156
  47.6 23.8 %collective-permute-start.11 = (f32[16,128,128]{2,1,0:T(8,128)S(1)}, f32[16,128,128]{2,1,0:T(8,128)S(1)}, u32[]{:S(2)}, u32[]{:S(2)}) collective-permute-start(f32[16,128,128]{2,1,0:T(8,128)S(1)} %relay_upwind_rows.3._), channel_id=1, source_target_pairs={{0,1},{1,0},{2,3},{3,2},{4,5},{5,4},{6,7},{7,6},{8,9},{9,8},{10,11... | collective-permute-start | bytes 3145736 | tf_op jit(solution)/shard_map/ppermute | solution.py:527
  60.1 17.1 %copy-start.7 = (f32[8,512]{1,0:T(8,128)S(1)}, f32[8,512]{1,0:T(8,128)}, u32[]{:S(2)}) copy-start(f32[8,512]{1,0:T(8,128)} %param.19) | copy-start | bytes 49156
  60.1 17.9 %copy-start.4 = (f32[64]{0:T(128)S(1)}, f32[64]{0:T(128)}, u32[]{:S(2)}) copy-start(f32[64]{0:T(128)} %refs_1_.7) | copy-start | bytes 772
  60.1 2.2 %collective-permute-start.7 = (f32[16,80,128]{2,1,0:T(8,128)S(1)}, f32[16,80,128]{2,1,0:T(8,128)S(1)}, u32[]{:S(2)}, u32[]{:S(2)}) collective-permute-start(f32[16,80,128]{2,1,0:T(8,128)S(1)} %get-tuple-element.74), channel_id=1, source_target_pairs={{0,8},{8,0},{16,24},{24,16},{1,9},{9,1},{17,25},{25,17},{2,10},{10... | collective-permute-start | bytes 1966088 | tf_op jit(solution)/shard_map/ppermute | solution.py:413
  62.3 10.6 %collective-permute-start.8 = (f32[17,16,128]{2,1,0:T(8,128)S(1)}, f32[17,16,128]{2,1,0:T(8,128)S(1)}, u32[]{:S(2)}, u32[]{:S(2)}) collective-permute-start(f32[17,16,128]{2,1,0:T(8,128)S(1)} %get-tuple-element.75), channel_id=1, source_target_pairs={{0,8},{8,0},{16,24},{24,16},{1,9},{9,1},{17,25},{25,17},{2,10},{10... | collective-permute-start | bytes 417800 | tf_op jit(solution)/shard_map/ppermute | solution.py:413
  62.5 10.8 %collective-permute-start.10 = (f32[17,16,128]{2,1,0:T(8,128)S(1)}, f32[17,16,128]{2,1,0:T(8,128)S(1)}, u32[]{:S(2)}, u32[]{:S(2)}) collective-permute-start(f32[17,16,128]{2,1,0:T(8,128)S(1)} %get-tuple-element.79), channel_id=1, source_target_pairs={{0,24},{8,16},{16,8},{24,0},{1,25},{9,17},{17,9},{25,1},{2,26},{10... | collective-permute-start | bytes 417800 | tf_op jit(solution)/shard_map/ppermute | solution.py:413
  62.8 10.5 %collective-permute-start.9 = (f32[17,16,128]{2,1,0:T(8,128)S(1)}, f32[17,16,128]{2,1,0:T(8,128)S(1)}, u32[]{:S(2)}, u32[]{:S(2)}) collective-permute-start(f32[17,16,128]{2,1,0:T(8,128)S(1)} %get-tuple-element.77), channel_id=1, source_target_pairs={{0,16},{8,24},{16,0},{24,8},{1,17},{9,25},{17,1},{25,9},{2,18},{10... | collective-permute-start | bytes 417800 | tf_op jit(solution)/shard_map/ppermute | solution.py:413
  71.4 17.1 %collective-permute-start.20 = (f32[16,32,128]{2,1,0:T(8,128)S(1)}, f32[16,32,128]{2,1,0:T(8,128)S(1)}, u32[]{:S(2)}, u32[]{:S(2)}) collective-permute-start(f32[16,32,128]{2,1,0:T(8,128)S(1)} %get-tuple-element.97), channel_id=1, source_target_pairs={{0,24},{8,16},{16,8},{24,0},{1,25},{9,17},{17,9},{25,1},{2,26},{10... | collective-permute-start | bytes 786440 | tf_op jit(solution)/shard_map/ppermute | solution.py:413
  71.4 18.1 %collective-permute-start.19 = (f32[16,32,128]{2,1,0:T(8,128)S(1)}, f32[16,32,128]{2,1,0:T(8,128)S(1)}, u32[]{:S(2)}, u32[]{:S(2)}) collective-permute-start(f32[16,32,128]{2,1,0:T(8,128)S(1)} %get-tuple-element.95), channel_id=1, source_target_pairs={{0,16},{8,24},{16,0},{24,8},{1,17},{9,25},{17,1},{25,9},{2,18},{10... | collective-permute-start | bytes 786440 | tf_op jit(solution)/shard_map/ppermute | solution.py:413
  72.9 4.5 %collective-permute-start.15 = (f32[16,32,128]{2,1,0:T(8,128)S(1)}, f32[16,32,128]{2,1,0:T(8,128)S(1)}, u32[]{:S(2)}, u32[]{:S(2)}) collective-permute-start(f32[16,32,128]{2,1,0:T(8,128)S(1)} %get-tuple-element.90), channel_id=1, source_target_pairs={{0,8},{8,0},{16,24},{24,16},{1,9},{9,1},{17,25},{25,17},{2,10},{10... | collective-permute-start | bytes 786440 | tf_op jit(solution)/shard_map/ppermute | solution.py:413
  75.6 12.9 %collective-permute-start.17 = (f32[16,16,128]{2,1,0:T(8,128)S(1)}, f32[16,16,128]{2,1,0:T(8,128)S(1)}, u32[]{:S(2)}, u32[]{:S(2)}) collective-permute-start(f32[16,16,128]{2,1,0:T(8,128)S(1)} %get-tuple-element.92), channel_id=1, source_target_pairs={{0,16},{8,24},{16,0},{24,8},{1,17},{9,25},{17,1},{25,9},{2,18},{10... | collective-permute-start | bytes 393224 | tf_op jit(solution)/shard_map/ppermute | solution.py:413
  77.3 18.2 %collective-permute-start.18 = (f32[16,16,128]{2,1,0:T(8,128)S(1)}, f32[16,16,128]{2,1,0:T(8,128)S(1)}, u32[]{:S(2)}, u32[]{:S(2)}) collective-permute-start(f32[16,16,128]{2,1,0:T(8,128)S(1)} %get-tuple-element.93), channel_id=1, source_target_pairs={{0,24},{8,16},{16,8},{24,0},{1,25},{9,17},{17,9},{25,1},{2,26},{10... | collective-permute-start | bytes 393224 | tf_op jit(solution)/shard_map/ppermute | solution.py:413
  77.4 18.1 %collective-permute-start.16 = (f32[16,16,128]{2,1,0:T(8,128)S(1)}, f32[16,16,128]{2,1,0:T(8,128)S(1)}, u32[]{:S(2)}, u32[]{:S(2)}) collective-permute-start(f32[16,16,128]{2,1,0:T(8,128)S(1)} %get-tuple-element.91), channel_id=1, source_target_pairs={{0,8},{8,0},{16,24},{24,16},{1,9},{9,1},{17,25},{25,17},{2,10},{10... | collective-permute-start | bytes 393224 | tf_op jit(solution)/shard_map/ppermute | solution.py:413
  88.5 10.2 %collective-permute-start.13 = (f32[16,16,128]{2,1,0:T(8,128)S(1)}, f32[16,16,128]{2,1,0:T(8,128)S(1)}, u32[]{:S(2)}, u32[]{:S(2)}) collective-permute-start(f32[16,16,128]{2,1,0:T(8,128)S(1)} %get-tuple-element.83), channel_id=1, source_target_pairs={{0,16},{8,24},{16,0},{24,8},{1,17},{9,25},{17,1},{25,9},{2,18},{10... | collective-permute-start | bytes 393224 | tf_op jit(solution)/shard_map/ppermute | solution.py:413
  88.5 10.2 %collective-permute-start.12 = (f32[16,16,128]{2,1,0:T(8,128)S(1)}, f32[16,16,128]{2,1,0:T(8,128)S(1)}, u32[]{:S(2)}, u32[]{:S(2)}) collective-permute-start(f32[16,16,128]{2,1,0:T(8,128)S(1)} %get-tuple-element.82), channel_id=1, source_target_pairs={{0,8},{8,0},{16,24},{24,16},{1,9},{9,1},{17,25},{25,17},{2,10},{10... | collective-permute-start | bytes 393224 | tf_op jit(solution)/shard_map/ppermute | solution.py:413
  89.4 9.3 %collective-permute-start.14 = (f32[16,16,128]{2,1,0:T(8,128)S(1)}, f32[16,16,128]{2,1,0:T(8,128)S(1)}, u32[]{:S(2)}, u32[]{:S(2)}) collective-permute-start(f32[16,16,128]{2,1,0:T(8,128)S(1)} %get-tuple-element.84), channel_id=1, source_target_pairs={{0,24},{8,16},{16,8},{24,0},{1,25},{9,17},{17,9},{25,1},{2,26},{10... | collective-permute-start | bytes 393224 | tf_op jit(solution)/shard_map/ppermute | solution.py:413
where the time goes:
time: 102 us
  waiting for transfers between devices  39.6 us (39%)
  Pallas kernels  39.5 us (39%)
  starting transfers between devices  20.1 us (20%)
  other arithmetic  1.14 us (1%)
    pallas_call x7, Pallas kernels, whole(): pl.pallas_call(kernel, in_specs=[smem] * 4 + [anywhere] + [vmem] * len(op...  18.5 us
    ppermute x15, waiting for transfers between devices, send(): lax.ppermute(after(parts[k], *events), 'sec', [(i, i ^ k) for i in range(...  16.7 us
    pallas_call x4, Pallas kernels, couple(): pl.pallas_call(functools.partial(couple_kernel, first, base, groups, grou...  14.8 us
    ppermute x3, waiting for transfers between devices, swapped(): return lax.ppermute(array, 'space', swap)  14.4 us
    ppermute x15, starting transfers between devices, send(): lax.ppermute(after(parts[k], *events), 'sec', [(i, i ^ k) for i in range(...  10.2 us
    ppermute x3, waiting for transfers between devices, hopped(): return lax.ppermute(array, 'space', pairs)  8.51 us
    ppermute x3, starting transfers between devices, hopped(): return lax.ppermute(array, 'space', pairs)  6.65 us
    pallas_call x1, Pallas kernels, sort(): pl.pallas_call(functools.partial(sort_kernel, outs, blocks), grid=(group_...  4.01 us
  transfers between devices with their start and end apart: 21, of which 8 were waited for; matrix products, arithmetic and copies ran while one was open for 0% of the time, Pallas kernels for 34%

commit v1 on v0

--- a/solution.py
+++ b/solution.py
@@ -545,7 +545,7 @@
         first = some[0] == 0
 
         in_specs = [smem] * 2 + [vmem] * (2 + 3 * groups)
-        operands = [place, evaporation_speed_stepwise, share, thermal]
+        operands = [place, evaporation_speed_stepwise, share, after(thermal, last) if first else thermal]
         operands += list(made.setdefault("sign", outer)) + list(inner) + list(outer)
         out_specs = [
             pl.BlockSpec(
@@ -597,22 +597,22 @@
     far_12 = hopped(after(near_12, relayed_0), outward)
     (relayed_34,) = relay(chosen_34, far_34, 1, after(relayed_0, near_0))
     near_34 = swapped(relayed_34)
-    outer_0 = transport_outer((0,), ((near_0,),), after(relayed_34, *far_in))
-    far_of_0 = send(outer_0, 2, groups, *far_in)
-    pair_in = send(inner, 1, 2, outer_0[0])
-    pair_of_0 = send(outer_0, 1, 2, far_12, *pair_in)
+    outer_0 = transport_outer((0,), ((near_0,),), after(relayed_34, far_in[-1]))
+    far_of_0 = [part for k in range(2, groups) for part in send(outer_0, k, k + 1, far_in[k - 2])]
+    pair_in = send(inner, 1, 2, outer_0[0], far_in[0])
+    pair_of_0 = send(outer_0, 1, 2, *pair_in)
     outer_12 = transport_outer(
-        (1, 2), ((near_12, far_12), (near_12, far_12)), outer_0[0], (0, 1)
+        (1, 2), ((near_12, far_12), (near_12, far_12)), after(outer_0[0], *far_of_0), (0, 1)
     )
-    far_of_12 = send(outer_12, 2, groups, near_34)
-    outer_3 = transport_outer((3,), ((near_34,),), after(outer_12[0], *far_of_0), (0,))
+    far_of_12 = send(outer_12, 2, 3) + send(outer_12, 3, groups, near_34)
+    sent = [inner[0], *pair_in, *far_in]
+    couple((0,), sent, 0, [outer_0[0], *pair_of_0, *far_of_0], far_of_12[0])
+    outer_3 = transport_outer((3,), ((near_34,),), made["merge"], (0,))
     far_of_3 = send(outer_3, 2, groups)
-    pair_of_12 = send(outer_12, 1, 2, *pair_of_0)
-    sent = [inner[0], *pair_in, *far_in]
-    couple((0,), sent, 0, [outer_0[0], *pair_of_0, *far_of_0], outer_3[0])
-    outer_4 = transport_outer((4,), ((near_34,),), made["merge"], (1,))
+    pair_of_12 = send(outer_12, 1, 2, near_34, *pair_of_0)
+    outer_4 = transport_outer((4,), ((near_34,),), outer_3[0], (1,))
     pair_of_3 = send(outer_3, 1, 2, *pair_of_12)
-    sent_4 = [outer_4[0]] + send(outer_4, 1, groups)
+    sent_4 = [outer_4[0]] + send(outer_4, 1, 2, *pair_of_3) + send(outer_4, 2, groups, *far_of_12)
     couple((1, 2), sent, 1, [outer_12[0], *pair_of_12, *far_of_12], outer_4[0])
     couple((3,), sent, 3, [outer_3[0], *pair_of_3, *far_of_3], outer_4[0])
     couple((4,), sent, 4, sent_4, outer_4[0])

time: 102 us -> 103 us (level)
  starting transfers between devices: 20.1 us -> 24.8 us
  waiting for transfers between devices: 39.6 us -> 35.2 us
    ppermute x3, waiting for transfers between devices: 8.51 us -> 0.87 us  [hopped(): return lax.ppermute(array, 'space', pairs)]
    ppermute x3, starting transfers between devices: 3.17 us -> 8.53 us  [swapped(): return lax.ppermute(array, 'space', swap)]
    ppermute x3, waiting for transfers between devices: 14.4 us -> 16.9 us  [swapped(): return lax.ppermute(array, 'space', swap)]
  transfers between devices with their start and end apart: 21 -> 21, of which waited for: 8 -> 8; matrix products, arithmetic and copies ran while one was open for 0% -> 0% of each run, Pallas kernels for 34% -> 33%
where the time goes in v1:
time: 103 us; the launch traced here: 102 us
  Pallas kernels  39.5 us (38%)
  waiting for transfers between devices  35.2 us (34%)
  starting transfers between devices  24.8 us (24%)
  other arithmetic  1.14 us (1%)
    pallas_call x7, Pallas kernels, whole(): pl.pallas_call(kernel, in_specs=[smem] * 4 + [anywhere] + [vmem] * len(op...  18.5 us
    ppermute x15, waiting for transfers between devices, send(): lax.ppermute(after(parts[k], *events), 'sec', [(i, i ^ k) for i in range(...  17.5 us
    ppermute x3, waiting for transfers between devices, swapped(): return lax.ppermute(array, 'space', swap)  16.9 us
    pallas_call x4, Pallas kernels, couple(): pl.pallas_call(functools.partial(couple_kernel, first, base, groups, grou...  14.9 us
    ppermute x15, starting transfers between devices, send(): lax.ppermute(after(parts[k], *events), 'sec', [(i, i ^ k) for i in range(...  10.2 us
    ppermute x3, starting transfers between devices, swapped(): return lax.ppermute(array, 'space', swap)  8.53 us
    ppermute x3, starting transfers between devices, hopped(): return lax.ppermute(array, 'space', pairs)  6.09 us
    pallas_call x1, Pallas kernels, sort(): pl.pallas_call(functools.partial(sort_kernel, outs, blocks), grid=(group_...  4 us
  transfers between devices with their start and end apart: 21, of which 8 were waited for; matrix products, arithmetic and copies ran while one was open for 0% of the time, Pallas kernels for 33%

profile of v1, /device:TPU:0, one launch (start us, length us, event | category | flops | bytes accessed | tf_op | source)
XLA Modules:
  0.0 102.3 jit_solution(6286304562573379532)
XLA Ops:
  0.6 0.1 pad_add_fusion.place_ref.refs_0_
  0.7 0.9 select_bitcast_fusion.refs_3_
  1.6 0.0 copy-start.1
  1.6 0.6 copy-done.1
  2.3 2.2 %select_upwind_rows.1 = (f32[18,64,128]{2,1,0:T(8,128)S(1)}, f32[16,128,128]{2,1,0:T(8,128)S(1)}, f32[128,128]{1,0:T(8,128)S(1)}) custom-call(f32[16]{0:T(128)S(1)} %copy-done.1, f32[16,640,128]{2,1,0:T(8,128)} %bitcast.34, f32[16,640,128]{2,1,0:T(8,128)} %bitcast.35, f32[16,640,128]{2,1,0:T(8,128)} %bitcast.36, f32[128,128]{1,0:T(8,128)S(1)} %select_bitcast_fusion.refs_3_), custom_call_target="tpu_custom_call" | custom-call | flops 3932160 | bytes 3932160 | tf_op jit(solution)/shard_map/select_upwind_rows/pallas_call | solution.py:428
  4.4 0.0 copy-start
  4.5 0.0 copy-start.3
  4.5 1.3 %collective-permute-start = (f32[18,64,128]{2,1,0:T(8,128)S(1)}, f32[18,64,128]{2,1,0:T(8,128)S(1)}, u32[]{:S(2)}, u32[]{:S(2)}) collective-permute-start(f32[18,64,128]{2,1,0:T(8,128)S(1)} %get-tuple-element.67.own_ref), channel_id=1, source_target_pairs={{2,0},{4,2},{6,4},{1,3},{3,5},{5,7},{10,8},{12,10},{14,12},{9,11},... | collective-permute-start | bytes 1769480 | tf_op jit(solution)/shard_map/ppermute | solution.py:530
  5.8 5.3 %collective-permute-start.9 = (f32[16,128,128]{2,1,0:T(8,128)S(1)}, f32[16,128,128]{2,1,0:T(8,128)S(1)}, u32[]{:S(2)}, u32[]{:S(2)}) collective-permute-start(f32[16,128,128]{2,1,0:T(8,128)S(1)} %get-tuple-element.82), channel_id=1, source_target_pairs={{0,1},{1,0},{2,3},{3,2},{4,5},{5,4},{6,7},{7,6},{8,9},{9,8},{10,11... | collective-permute-start | bytes 3145736 | tf_op jit(solution)/shard_map/ppermute | solution.py:527
  11.0 4.0 %sort_cells.1 = (f32[16,128,128]{2,1,0:T(8,128)S(1)}, f32[16,128,128]{2,1,0:T(8,128)S(1)}, f32[16,128,128]{2,1,0:T(8,128)S(1)}, f32[16,128,128]{2,1,0:T(8,128)S(...) custom-call(f32[16]{0:T(128)S(1)} %copy-done.2, f32[16,640,128]{2,1,0:T(8,128)} %bitcast.37), custom_call_target="tpu_custom_call" | custom-call | flops 6553600 | bytes 6553600 | tf_op jit(solution)/shard_map/sort_cells/pallas_call | solution.py:448
  15.0 1.3 %collective-permute-start.2 = (f32[16,128,128]{2,1,0:T(8,128)S(1)}, f32[16,128,128]{2,1,0:T(8,128)S(1)}, u32[]{:S(2)}, u32[]{:S(2)}) collective-permute-start(f32[16,128,128]{2,1,0:T(8,128)S(1)} %get-tuple-element.60._.own_ref), channel_id=1, source_target_pairs={{2,0},{4,2},{6,4},{1,3},{3,5},{5,7},{10,8},{12,10},{14,12},{9,11},... | collective-permute-start | bytes 3145736 | tf_op jit(solution)/shard_map/ppermute | solution.py:530
  16.3 6.3 %transport_inner_rows.1 = (f32[16,80,128]{2,1,0:T(8,128)S(1)}, f32[16,80,128]{2,1,0:T(8,128)S(1)}, f32[16,80,128]{2,1,0:T(8,128)S(1)}, f32[16,80,128]{2,1,0:T(8,128)S(1)}) custom-call(s32[2]{0:T(128)S(1)} %pad_add_fusion.place_ref.refs_0_, f32[16]{0:T(128)S(1)} %copy-done.2, f32[16]{0:T(128)S(1)} %copy-done.3, f32[5,16]{1,0:T(8,128)S(1)} %bitcast.27, ...), custom_call_target="tpu_custom_call" | custom-call | flops 6553600 | bytes 6553600 | tf_op jit(solution)/shard_map/transport_inner_rows/pallas_call | solution.py:468
  22.7 0.9 collective-permute-done.far_ref
  23.5 0.9 relay_upwind_rows.2._
  24.5 1.5 %collective-permute-start.1 = (f32[18,64,128]{2,1,0:T(8,128)S(1)}, f32[18,64,128]{2,1,0:T(8,128)S(1)}, u32[]{:S(2)}, u32[]{:S(2)}) collective-permute-start(f32[18,64,128]{2,1,0:T(8,128)S(1)} %relay_upwind_rows.2._), channel_id=1, source_target_pairs={{0,1},{1,0},{2,3},{3,2},{4,5},{5,4},{6,7},{7,6},{8,9},{9,8},{10,11... | collective-permute-start | bytes 1769480 | tf_op jit(solution)/shard_map/ppermute | solution.py:527
  26.0 0.1 collective-permute-start.3
  26.0 1.4 %collective-permute-start.4 = (f32[16,80,128]{2,1,0:T(8,128)S(1)}, f32[16,80,128]{2,1,0:T(8,128)S(1)}, u32[]{:S(2)}, u32[]{:S(2)}) collective-permute-start(f32[16,80,128]{2,1,0:T(8,128)S(1)} %get-tuple-element.74), channel_id=1, source_target_pairs={{0,16},{8,24},{16,0},{24,8},{1,17},{9,25},{17,1},{25,9},{2,18},{10... | collective-permute-start | bytes 1966088 | tf_op jit(solution)/shard_map/ppermute | solution.py:413
  27.5 7.6 %collective-permute-done.9.rest_2_.rest_4_ = f32[16,128,128]{2,1,0:T(8,128)S(1)} collective-permute-done((f32[16,128,128]{2,1,0:T(8,128)S(1)}, f32[16,128,128]{2,1,0:T(8,128)S(1)}, u32[]{:S(2)}, u32[]{:S(2)}) %collective-permute-start.9) | collective-permute-done | bytes 1048608 | tf_op jit(solution)/shard_map/ppermute | solution.py:527
  35.0 3.5 %collective-permute-start.10 = (f32[16,128,128]{2,1,0:T(8,128)S(1)}, f32[16,128,128]{2,1,0:T(8,128)S(1)}, u32[]{:S(2)}, u32[]{:S(2)}) collective-permute-start(f32[16,128,128]{2,1,0:T(8,128)S(1)} %collective-permute-done.9.rest_2_.rest_4_), channel_id=1, source_target_pairs={{0,2},{2,4},{4,6},{3,1},{5,3},{7,5},{8,10},{10,12},{12,14},{11,9},... | collective-permute-start | bytes 3145736 | tf_op jit(solution)/shard_map/ppermute | solution.py:530
  38.6 8.0 %collective-permute-done.1.edge_ref.rest_1_ = f32[18,64,128]{2,1,0:T(8,128)S(1)} collective-permute-done((f32[18,64,128]{2,1,0:T(8,128)S(1)}, f32[18,64,128]{2,1,0:T(8,128)S(1)}, u32[]{:S(2)}, u32[]{:S(2)}) %collective-permute-start.1) | collective-permute-done | bytes 589856 | tf_op jit(solution)/shard_map/ppermute | solution.py:527
  46.5 1.0 relay_upwind_rows.3._
  47.5 1.8 %collective-permute-start.12 = (f32[16,128,128]{2,1,0:T(8,128)S(1)}, f32[16,128,128]{2,1,0:T(8,128)S(1)}, u32[]{:S(2)}, u32[]{:S(2)}) collective-permute-start(f32[16,128,128]{2,1,0:T(8,128)S(1)} %relay_upwind_rows.3._), channel_id=1, source_target_pairs={{0,1},{1,0},{2,3},{3,2},{4,5},{5,4},{6,7},{7,6},{8,9},{9,8},{10,11... | collective-permute-start | bytes 3145736 | tf_op jit(solution)/shard_map/ppermute | solution.py:527
  49.4 2.3 %transport_outer_rows.4 = (f32[17,16,128]{2,1,0:T(8,128)S(1)}, f32[17,16,128]{2,1,0:T(8,128)S(1)}, f32[17,16,128]{2,1,0:T(8,128)S(1)}, f32[17,16,128]{2,1,0:T(8,128)S(1)}) custom-call(s32[2]{0:T(128)S(1)} %pad_add_fusion.place_ref.refs_0_, f32[16]{0:T(128)S(1)} %copy-done.2, f32[16]{0:T(128)S(1)} %copy-done.3, f32[5,16]{1,0:T(8,128)S(1)} %bitcast.30, ...), custom_call_target="tpu_custom_call" | custom-call | flops 1310720 | bytes 1310720 | tf_op jit(solution)/shard_map/transport_outer_rows/pallas_call | solution.py:468
  51.7 5.4 %collective-permute-done.4.refs_10_ = f32[16,80,128]{2,1,0:T(8,128)S(1)} collective-permute-done((f32[16,80,128]{2,1,0:T(8,128)S(1)}, f32[16,80,128]{2,1,0:T(8,128)S(1)}, u32[]{:S(2)}, u32[]{:S(2)}) %collective-permute-start.4) | collective-permute-done | bytes 655392 | tf_op jit(solution)/shard_map/ppermute | solution.py:413
  57.0 0.1 collective-permute-start.5
  57.1 0.3 collective-permute-start.8
  57.4 1.8 %collective-permute-start.7 = (f32[17,16,128]{2,1,0:T(8,128)S(1)}, f32[17,16,128]{2,1,0:T(8,128)S(1)}, u32[]{:S(2)}, u32[]{:S(2)}) collective-permute-start(f32[17,16,128]{2,1,0:T(8,128)S(1)} %get-tuple-element.78), channel_id=1, source_target_pairs={{0,16},{8,24},{16,0},{24,8},{1,17},{9,25},{17,1},{25,9},{2,18},{10... | collective-permute-start | bytes 417800 | tf_op jit(solution)/shard_map/ppermute | solution.py:413
  59.2 0.1 collective-permute-start.6
  59.3 3.2 %collective-permute-done.8.refs_7_.refs_15_ = f32[17,16,128]{2,1,0:T(8,128)S(1)} collective-permute-done((f32[17,16,128]{2,1,0:T(8,128)S(1)}, f32[17,16,128]{2,1,0:T(8,128)S(1)}, u32[]{:S(2)}, u32[]{:S(2)}) %collective-permute-start.8) | collective-permute-done | bytes 139296 | tf_op jit(solution)/shard_map/ppermute | solution.py:413
  62.5 3.5 %collective-permute-done.7.refs_6_.refs_14_ = f32[17,16,128]{2,1,0:T(8,128)S(1)} collective-permute-done((f32[17,16,128]{2,1,0:T(8,128)S(1)}, f32[17,16,128]{2,1,0:T(8,128)S(1)}, u32[]{:S(2)}, u32[]{:S(2)}) %collective-permute-start.7) | collective-permute-done | bytes 139296 | tf_op jit(solution)/shard_map/ppermute | solution.py:413
  66.1 3.4 %transport_outer_rows.5 = (f32[16,32,128]{2,1,0:T(8,128)S(1)}, f32[16,32,128]{2,1,0:T(8,128)S(1)}, f32[16,32,128]{2,1,0:T(8,128)S(1)}, f32[16,32,128]{2,1,0:T(8,128)S(1)}) custom-call(s32[2]{0:T(128)S(1)} %pad_add_fusion.place_ref.refs_0_, f32[16]{0:T(128)S(1)} %copy-done.2, f32[16]{0:T(128)S(1)} %copy-done.3, f32[5,16]{1,0:T(8,128)S(1)} %bitcast.31, ...), custom_call_target="tpu_custom_call" | custom-call | flops 2621440 | bytes 2621440 | tf_op jit(solution)/shard_map/transport_outer_rows/pallas_call | solution.py:468
  69.5 0.8 collective-permute-start.11
  70.3 1.4 %collective-permute-done.12.rest_1_ = f32[16,128,128]{2,1,0:T(8,128)S(1)} collective-permute-done((f32[16,128,128]{2,1,0:T(8,128)S(1)}, f32[16,128,128]{2,1,0:T(8,128)S(1)}, u32[]{:S(2)}, u32[]{:S(2)}) %collective-permute-start.12) | collective-permute-done | bytes 1048608 | tf_op jit(solution)/shard_map/ppermute | solution.py:527
  71.7 1.7 %collective-permute-start.16 = (f32[16,32,128]{2,1,0:T(8,128)S(1)}, f32[16,32,128]{2,1,0:T(8,128)S(1)}, u32[]{:S(2)}, u32[]{:S(2)}) collective-permute-start(f32[16,32,128]{2,1,0:T(8,128)S(1)} %get-tuple-element.97), channel_id=1, source_target_pairs={{0,24},{8,16},{16,8},{24,0},{1,25},{9,17},{17,9},{25,1},{2,26},{10... | collective-permute-start | bytes 786440 | tf_op jit(solution)/shard_map/ppermute | solution.py:413
  73.3 0.1 pad_maximum_fusion.1.refs_16_
  73.4 0.1 pad_maximum_fusion.refs_2_
  73.5 5.3 %collective-permute-done.11.refs_14_ = f32[16,32,128]{2,1,0:T(8,128)S(1)} collective-permute-done((f32[16,32,128]{2,1,0:T(8,128)S(1)}, f32[16,32,128]{2,1,0:T(8,128)S(1)}, u32[]{:S(2)}, u32[]{:S(2)}) %collective-permute-start.11) | collective-permute-done | bytes 262176 | tf_op jit(solution)/shard_map/ppermute | solution.py:413
  78.8 3.6 %couple_sections.4 = (f32[64,160,128]{2,1,0:T(8,128)}, f32[5,8,512]{2,1,0:T(8,128)}, f32[8,64,512]{2,1,0:T(8,128)S(1)}) custom-call(s32[2]{0:T(128)S(1)} %pad_add_fusion.place_ref.refs_0_, f32[64]{0:T(128)S(1)} %copy-done.4, bf16[64,192]{1,0:T(8,128)(2,1)S(1)} %pad_maximum_fusion.refs_2_, f32[32,128]{1,0:T(8,128)S(1)} %bitcast.23, ...), custom_call_target="tpu_custom_call" | custom-call | flops 33554432 | bytes 3145728 | tf_op jit(solution)/shard_map/couple_sections/pallas_call | solution.py:567
  82.4 2.3 %transport_outer_rows.6 = (f32[16,16,128]{2,1,0:T(8,128)S(1)}, f32[16,16,128]{2,1,0:T(8,128)S(1)}, f32[16,16,128]{2,1,0:T(8,128)S(1)}, f32[16,16,128]{2,1,0:T(8,128)S(1)}) custom-call(s32[2]{0:T(128)S(1)} %pad_add_fusion.place_ref.refs_0_, f32[16]{0:T(128)S(1)} %copy-done.2, f32[16]{0:T(128)S(1)} %copy-done.3, f32[5,16]{1,0:T(8,128)S(1)} %bitcast.32, ...), custom_call_target="tpu_custom_call" | custom-call | flops 1310720 | bytes 1310720 | tf_op jit(solution)/shard_map/transport_outer_rows/pallas_call | solution.py:468
  84.7 0.1 collective-permute-start.14
  84.7 0.7 collective-permute-start.19
  85.5 1.1 %collective-permute-start.20 = (f32[16,16,128]{2,1,0:T(8,128)S(1)}, f32[16,16,128]{2,1,0:T(8,128)S(1)}, u32[]{:S(2)}, u32[]{:S(2)}) collective-permute-start(f32[16,16,128]{2,1,0:T(8,128)S(1)} %get-tuple-element.102), channel_id=1, source_target_pairs={{0,24},{8,16},{16,8},{24,0},{1,25},{9,17},{17,9},{25,1},{2,26},{10... | collective-permute-start | bytes 393224 | tf_op jit(solution)/shard_map/ppermute | solution.py:413
  86.6 2.3 %transport_outer_rows.7 = (f32[16,16,128]{2,1,0:T(8,128)S(1)}, f32[16,16,128]{2,1,0:T(8,128)S(1)}, f32[16,16,128]{2,1,0:T(8,128)S(1)}, f32[16,16,128]{2,1,0:T(8,128)S(1)}) custom-call(s32[2]{0:T(128)S(1)} %pad_add_fusion.place_ref.refs_0_, f32[16]{0:T(128)S(1)} %copy-done.2, f32[16]{0:T(128)S(1)} %copy-done.3, f32[5,16]{1,0:T(8,128)S(1)} %bitcast.33, ...), custom_call_target="tpu_custom_call" | custom-call | flops 1310720 | bytes 1310720 | tf_op jit(solution)/shard_map/transport_outer_rows/pallas_call | solution.py:468
  88.9 0.7 collective-permute-start.18
  89.6 1.4 %collective-permute-start.17 = (f32[16,16,128]{2,1,0:T(8,128)S(1)}, f32[16,16,128]{2,1,0:T(8,128)S(1)}, u32[]{:S(2)}, u32[]{:S(2)}) collective-permute-start(f32[16,16,128]{2,1,0:T(8,128)S(1)} %get-tuple-element.98), channel_id=1, source_target_pairs={{0,16},{8,24},{16,0},{24,8},{1,17},{9,25},{17,1},{25,9},{2,18},{10... | collective-permute-start | bytes 393224 | tf_op jit(solution)/shard_map/ppermute | solution.py:413
  91.0 5.0 %couple_sections.5 = (f32[64,160,128]{2,1,0:T(8,128)}, f32[5,8,512]{2,1,0:T(8,128)}) custom-call(s32[2]{0:T(128)S(1)} %pad_add_fusion.place_ref.refs_0_, f32[64]{0:T(128)S(1)} %copy-done.4, bf16[64,192]{1,0:T(8,128)(2,1)S(1)} %pad_maximum_fusion.refs_2_, f32[32,128]{1,0:T(8,128)S(1)} %bitcast.24, ...), custom_call_target="tpu_custom_call", output_to_operand_aliasing={{0}: (17, {}), {1}: (18, {})} | custom-call | flops 67108864 | bytes 6291456 | tf_op jit(solution)/shard_map/couple_sections/pallas_call | solution.py:567
  95.9 3.2 %couple_sections.6 = (f32[64,160,128]{2,1,0:T(8,128)}, f32[5,8,512]{2,1,0:T(8,128)}) custom-call(s32[2]{0:T(128)S(1)} %pad_add_fusion.place_ref.refs_0_, f32[64]{0:T(128)S(1)} %copy-done.4, bf16[64,192]{1,0:T(8,128)(2,1)S(1)} %pad_maximum_fusion.refs_2_, f32[32,128]{1,0:T(8,128)S(1)} %bitcast.25, ...), custom_call_target="tpu_custom_call", output_to_operand_aliasing={{0}: (17, {}), {1}: (18, {})} | custom-call | flops 33554432 | bytes 3145728 | tf_op jit(solution)/shard_map/couple_sections/pallas_call | solution.py:567
  99.1 3.2 %couple_sections.7 = (f32[64,160,128]{2,1,0:T(8,128)}, f32[5,8,512]{2,1,0:T(8,128)}) custom-call(s32[2]{0:T(128)S(1)} %pad_add_fusion.place_ref.refs_0_, f32[64]{0:T(128)S(1)} %copy-done.4, bf16[64,192]{1,0:T(8,128)(2,1)S(1)} %pad_maximum_fusion.refs_2_, f32[32,128]{1,0:T(8,128)S(1)} %bitcast.26, ...), custom_call_target="tpu_custom_call", output_to_operand_aliasing={{0}: (17, {}), {1}: (18, {})} | custom-call | flops 33554432 | bytes 3145728 | tf_op jit(solution)/shard_map/couple_sections/pallas_call | solution.py:567
  (30 shorter events, 0.1 us)
Async XLA Ops:
  1.6 0.7 copy-start.1
  2.3 8.8 %copy-start.2 = (f32[16]{0:T(128)S(1)}, f32[16]{0:T(128)}, u32[]{:S(2)}) copy-start(f32[16]{0:T(128)} %ux_ref.15) | copy-start | bytes 196
  4.4 11.9 %copy-start = (f32[16,5]{0,1:T(8,128)S(1)}, f32[16,5]{0,1:T(8,128)}, u32[]{:S(2)}) copy-start(f32[16,5]{0,1:T(8,128)} %param.13) | copy-start | bytes 964
  4.5 11.9 %copy-start.3 = (f32[16]{0:T(128)S(1)}, f32[16]{0:T(128)}, u32[]{:S(2)}) copy-start(f32[16]{0:T(128)} %uy_ref.13) | copy-start | bytes 196
  4.5 19.1 %collective-permute-start = (f32[18,64,128]{2,1,0:T(8,128)S(1)}, f32[18,64,128]{2,1,0:T(8,128)S(1)}, u32[]{:S(2)}, u32[]{:S(2)}) collective-permute-start(f32[18,64,128]{2,1,0:T(8,128)S(1)} %get-tuple-element.67.own_ref), channel_id=1, source_target_pairs={{2,0},{4,2},{6,4},{1,3},{3,5},{5,7},{10,8},{12,10},{14,12},{9,11},... | collective-permute-start | bytes 1769480 | tf_op jit(solution)/shard_map/ppermute | solution.py:530
  5.8 29.3 %collective-permute-start.9 = (f32[16,128,128]{2,1,0:T(8,128)S(1)}, f32[16,128,128]{2,1,0:T(8,128)S(1)}, u32[]{:S(2)}, u32[]{:S(2)}) collective-permute-start(f32[16,128,128]{2,1,0:T(8,128)S(1)} %get-tuple-element.82), channel_id=1, source_target_pairs={{0,1},{1,0},{2,3},{3,2},{4,5},{5,4},{6,7},{7,6},{8,9},{9,8},{10,11... | collective-permute-start | bytes 3145736 | tf_op jit(solution)/shard_map/ppermute | solution.py:527
  15.0 31.5 %collective-permute-start.2 = (f32[16,128,128]{2,1,0:T(8,128)S(1)}, f32[16,128,128]{2,1,0:T(8,128)S(1)}, u32[]{:S(2)}, u32[]{:S(2)}) collective-permute-start(f32[16,128,128]{2,1,0:T(8,128)S(1)} %get-tuple-element.60._.own_ref), channel_id=1, source_target_pairs={{2,0},{4,2},{6,4},{1,3},{3,5},{5,7},{10,8},{12,10},{14,12},{9,11},... | collective-permute-start | bytes 3145736 | tf_op jit(solution)/shard_map/ppermute | solution.py:530
  22.7 36.6 %copy-start.5 = (f32[64,64]{1,0:T(8,128)S(1)}, f32[64,64]{1,0:T(8,128)}, u32[]{:S(2)}) copy-start(f32[64,64]{1,0:T(8,128)} %param.16) | copy-start | bytes 49156
  24.5 22.0 %collective-permute-start.1 = (f32[18,64,128]{2,1,0:T(8,128)S(1)}, f32[18,64,128]{2,1,0:T(8,128)S(1)}, u32[]{:S(2)}, u32[]{:S(2)}) collective-permute-start(f32[18,64,128]{2,1,0:T(8,128)S(1)} %relay_upwind_rows.2._), channel_id=1, source_target_pairs={{0,1},{1,0},{2,3},{3,2},{4,5},{5,4},{6,7},{7,6},{8,9},{9,8},{10,11... | collective-permute-start | bytes 1769480 | tf_op jit(solution)/shard_map/ppermute | solution.py:527
  26.0 23.4 %collective-permute-start.3 = (f32[16,80,128]{2,1,0:T(8,128)S(1)}, f32[16,80,128]{2,1,0:T(8,128)S(1)}, u32[]{:S(2)}, u32[]{:S(2)}) collective-permute-start(f32[16,80,128]{2,1,0:T(8,128)S(1)} %get-tuple-element.69), channel_id=1, source_target_pairs={{0,24},{8,16},{16,8},{24,0},{1,25},{9,17},{17,9},{25,1},{2,26},{10... | collective-permute-start | bytes 1966088 | tf_op jit(solution)/shard_map/ppermute | solution.py:413
  26.0 31.0 %collective-permute-start.4 = (f32[16,80,128]{2,1,0:T(8,128)S(1)}, f32[16,80,128]{2,1,0:T(8,128)S(1)}, u32[]{:S(2)}, u32[]{:S(2)}) collective-permute-start(f32[16,80,128]{2,1,0:T(8,128)S(1)} %get-tuple-element.74), channel_id=1, source_target_pairs={{0,16},{8,24},{16,0},{24,8},{1,17},{9,25},{17,1},{25,9},{2,18},{10... | collective-permute-start | bytes 1966088 | tf_op jit(solution)/shard_map/ppermute | solution.py:413
  35.0 31.0 %collective-permute-start.10 = (f32[16,128,128]{2,1,0:T(8,128)S(1)}, f32[16,128,128]{2,1,0:T(8,128)S(1)}, u32[]{:S(2)}, u32[]{:S(2)}) collective-permute-start(f32[16,128,128]{2,1,0:T(8,128)S(1)} %collective-permute-done.9.rest_2_.rest_4_), channel_id=1, source_target_pairs={{0,2},{2,4},{4,6},{3,1},{5,3},{7,5},{8,10},{10,12},{12,14},{11,9},... | collective-permute-start | bytes 3145736 | tf_op jit(solution)/shard_map/ppermute | solution.py:530
  47.5 24.1 %copy-start.6 = (f32[64,64]{1,0:T(8,128)S(1)}, f32[64,64]{1,0:T(8,128)}, u32[]{:S(2)}) copy-start(f32[64,64]{1,0:T(8,128)} %param.17) | copy-start | bytes 49156
  47.5 25.9 %copy-start.7 = (f32[8,512]{1,0:T(8,128)S(1)}, f32[8,512]{1,0:T(8,128)}, u32[]{:S(2)}) copy-start(f32[8,512]{1,0:T(8,128)} %param.19) | copy-start | bytes 49156
  47.5 31.3 %copy-start.4 = (f32[64]{0:T(128)S(1)}, f32[64]{0:T(128)}, u32[]{:S(2)}) copy-start(f32[64]{0:T(128)} %refs_1_.7) | copy-start | bytes 772
  47.5 24.1 %collective-permute-start.12 = (f32[16,128,128]{2,1,0:T(8,128)S(1)}, f32[16,128,128]{2,1,0:T(8,128)S(1)}, u32[]{:S(2)}, u32[]{:S(2)}) collective-permute-start(f32[16,128,128]{2,1,0:T(8,128)S(1)} %relay_upwind_rows.3._), channel_id=1, source_target_pairs={{0,1},{1,0},{2,3},{3,2},{4,5},{5,4},{6,7},{7,6},{8,9},{9,8},{10,11... | collective-permute-start | bytes 3145736 | tf_op jit(solution)/shard_map/ppermute | solution.py:527
  57.0 2.1 %collective-permute-start.5 = (f32[16,80,128]{2,1,0:T(8,128)S(1)}, f32[16,80,128]{2,1,0:T(8,128)S(1)}, u32[]{:S(2)}, u32[]{:S(2)}) collective-permute-start(f32[16,80,128]{2,1,0:T(8,128)S(1)} %get-tuple-element.75), channel_id=1, source_target_pairs={{0,8},{8,0},{16,24},{24,16},{1,9},{9,1},{17,25},{25,17},{2,10},{10... | collective-permute-start | bytes 1966088 | tf_op jit(solution)/shard_map/ppermute | solution.py:413
  57.1 5.4 %collective-permute-start.8 = (f32[17,16,128]{2,1,0:T(8,128)S(1)}, f32[17,16,128]{2,1,0:T(8,128)S(1)}, u32[]{:S(2)}, u32[]{:S(2)}) collective-permute-start(f32[17,16,128]{2,1,0:T(8,128)S(1)} %get-tuple-element.80), channel_id=1, source_target_pairs={{0,24},{8,16},{16,8},{24,0},{1,25},{9,17},{17,9},{25,1},{2,26},{10... | collective-permute-start | bytes 417800 | tf_op jit(solution)/shard_map/ppermute | solution.py:413
  57.4 8.6 %collective-permute-start.7 = (f32[17,16,128]{2,1,0:T(8,128)S(1)}, f32[17,16,128]{2,1,0:T(8,128)S(1)}, u32[]{:S(2)}, u32[]{:S(2)}) collective-permute-start(f32[17,16,128]{2,1,0:T(8,128)S(1)} %get-tuple-element.78), channel_id=1, source_target_pairs={{0,16},{8,24},{16,0},{24,8},{1,17},{9,25},{17,1},{25,9},{2,18},{10... | collective-permute-start | bytes 417800 | tf_op jit(solution)/shard_map/ppermute | solution.py:413
  59.2 11.1 %collective-permute-start.6 = (f32[17,16,128]{2,1,0:T(8,128)S(1)}, f32[17,16,128]{2,1,0:T(8,128)S(1)}, u32[]{:S(2)}, u32[]{:S(2)}) collective-permute-start(f32[17,16,128]{2,1,0:T(8,128)S(1)} %get-tuple-element.76), channel_id=1, source_target_pairs={{0,8},{8,0},{16,24},{24,16},{1,9},{9,1},{17,25},{25,17},{2,10},{10... | collective-permute-start | bytes 417800 | tf_op jit(solution)/shard_map/ppermute | solution.py:413
  69.5 9.3 %collective-permute-start.11 = (f32[16,32,128]{2,1,0:T(8,128)S(1)}, f32[16,32,128]{2,1,0:T(8,128)S(1)}, u32[]{:S(2)}, u32[]{:S(2)}) collective-permute-start(f32[16,32,128]{2,1,0:T(8,128)S(1)} %get-tuple-element.84), channel_id=1, source_target_pairs={{0,16},{8,24},{16,0},{24,8},{1,17},{9,25},{17,1},{25,9},{2,18},{10... | collective-permute-start | bytes 786440 | tf_op jit(solution)/shard_map/ppermute | solution.py:413
  71.6 13.0 %collective-permute-start.13 = (f32[16,32,128]{2,1,0:T(8,128)S(1)}, f32[16,32,128]{2,1,0:T(8,128)S(1)}, u32[]{:S(2)}, u32[]{:S(2)}) collective-permute-start(f32[16,32,128]{2,1,0:T(8,128)S(1)} %get-tuple-element.92), channel_id=1, source_target_pairs={{0,8},{8,0},{16,24},{24,16},{1,9},{9,1},{17,25},{25,17},{2,10},{10... | collective-permute-start | bytes 786440 | tf_op jit(solution)/shard_map/ppermute | solution.py:413
  71.7 17.2 %collective-permute-start.16 = (f32[16,32,128]{2,1,0:T(8,128)S(1)}, f32[16,32,128]{2,1,0:T(8,128)S(1)}, u32[]{:S(2)}, u32[]{:S(2)}) collective-permute-start(f32[16,32,128]{2,1,0:T(8,128)S(1)} %get-tuple-element.97), channel_id=1, source_target_pairs={{0,24},{8,16},{16,8},{24,0},{1,25},{9,17},{17,9},{25,1},{2,26},{10... | collective-permute-start | bytes 786440 | tf_op jit(solution)/shard_map/ppermute | solution.py:413
  84.7 6.3 %collective-permute-start.14 = (f32[16,16,128]{2,1,0:T(8,128)S(1)}, f32[16,16,128]{2,1,0:T(8,128)S(1)}, u32[]{:S(2)}, u32[]{:S(2)}) collective-permute-start(f32[16,16,128]{2,1,0:T(8,128)S(1)} %get-tuple-element.93), channel_id=1, source_target_pairs={{0,8},{8,0},{16,24},{24,16},{1,9},{9,1},{17,25},{25,17},{2,10},{10... | collective-permute-start | bytes 393224 | tf_op jit(solution)/shard_map/ppermute | solution.py:413
  84.7 11.2 %collective-permute-start.19 = (f32[16,16,128]{2,1,0:T(8,128)S(1)}, f32[16,16,128]{2,1,0:T(8,128)S(1)}, u32[]{:S(2)}, u32[]{:S(2)}) collective-permute-start(f32[16,16,128]{2,1,0:T(8,128)S(1)} %get-tuple-element.101), channel_id=1, source_target_pairs={{0,16},{8,24},{16,0},{24,8},{1,17},{9,25},{17,1},{25,9},{2,18},{10... | collective-permute-start | bytes 393224 | tf_op jit(solution)/shard_map/ppermute | solution.py:413
  85.5 10.5 %collective-permute-start.20 = (f32[16,16,128]{2,1,0:T(8,128)S(1)}, f32[16,16,128]{2,1,0:T(8,128)S(1)}, u32[]{:S(2)}, u32[]{:S(2)}) collective-permute-start(f32[16,16,128]{2,1,0:T(8,128)S(1)} %get-tuple-element.102), channel_id=1, source_target_pairs={{0,24},{8,16},{16,8},{24,0},{1,25},{9,17},{17,9},{25,1},{2,26},{10... | collective-permute-start | bytes 393224 | tf_op jit(solution)/shard_map/ppermute | solution.py:413
  88.9 10.2 %collective-permute-start.18 = (f32[16,16,128]{2,1,0:T(8,128)S(1)}, f32[16,16,128]{2,1,0:T(8,128)S(1)}, u32[]{:S(2)}, u32[]{:S(2)}) collective-permute-start(f32[16,16,128]{2,1,0:T(8,128)S(1)} %get-tuple-element.100), channel_id=1, source_target_pairs={{0,24},{8,16},{16,8},{24,0},{1,25},{9,17},{17,9},{25,1},{2,26},{10... | collective-permute-start | bytes 393224 | tf_op jit(solution)/shard_map/ppermute | solution.py:413
  89.6 9.5 %collective-permute-start.17 = (f32[16,16,128]{2,1,0:T(8,128)S(1)}, f32[16,16,128]{2,1,0:T(8,128)S(1)}, u32[]{:S(2)}, u32[]{:S(2)}) collective-permute-start(f32[16,16,128]{2,1,0:T(8,128)S(1)} %get-tuple-element.98), channel_id=1, source_target_pairs={{0,16},{8,24},{16,0},{24,8},{1,17},{9,25},{17,1},{25,9},{2,18},{10... | collective-permute-start | bytes 393224 | tf_op jit(solution)/shard_map/ppermute | solution.py:413
  90.9 8.2 %collective-permute-start.15 = (f32[16,16,128]{2,1,0:T(8,128)S(1)}, f32[16,16,128]{2,1,0:T(8,128)S(1)}, u32[]{:S(2)}, u32[]{:S(2)}) collective-permute-start(f32[16,16,128]{2,1,0:T(8,128)S(1)} %get-tuple-element.94), channel_id=1, source_target_pairs={{0,8},{8,0},{16,24},{24,16},{1,9},{9,1},{17,25},{25,17},{2,10},{10... | collective-permute-start | bytes 393224 | tf_op jit(solution)/shard_map/ppermute | solution.py:413

commit v2 on v1

--- a/solution.py
+++ b/solution.py
@@ -606,8 +606,8 @@
     )
     far_of_12 = send(outer_12, 2, 3) + send(outer_12, 3, groups, near_34)
     sent = [inner[0], *pair_in, *far_in]
-    couple((0,), sent, 0, [outer_0[0], *pair_of_0, *far_of_0], far_of_12[0])
-    outer_3 = transport_outer((3,), ((near_34,),), made["merge"], (0,))
+    couple((0,), sent, 0, [outer_0[0], *pair_of_0, *far_of_0], outer_12[0])
+    outer_3 = transport_outer((3,), ((near_34,),), after(made["merge"], far_of_12[0]), (0,))
     far_of_3 = send(outer_3, 2, groups)
     pair_of_12 = send(outer_12, 1, 2, near_34, *pair_of_0)
     outer_4 = transport_outer((4,), ((near_34,),), outer_3[0], (1,))

time: 103 us -> 98.6 us (0.957)
  waiting for transfers between devices: 35.2 us -> 32 us
    ppermute x15, waiting for transfers between devices: 17.5 us -> 13.1 us  [send(): lax.ppermute(after(parts[k], *events), 'sec', [(i, i ^ k) for i in range(...]
    ppermute x3, waiting for transfers between devices: 16.9 us -> 18 us  [swapped(): return lax.ppermute(array, 'space', swap)]
  transfers between devices with their start and end apart: 21 -> 21, of which waited for: 8 -> 9; matrix products, arithmetic and copies ran while one was open for 0% -> 0% of each run, Pallas kernels for 33% -> 35%
where the time goes in v2:
time: 98.6 us; the launch traced here: 98.3 us
  Pallas kernels  39.5 us (40%)
  waiting for transfers between devices  32 us (32%)
  starting transfers between devices  24 us (24%)
  other arithmetic  1.14 us (1%)
    pallas_call x7, Pallas kernels, whole(): pl.pallas_call(kernel, in_specs=[smem] * 4 + [anywhere] + [vmem] * len(op...  18.5 us
    ppermute x3, waiting for transfers between devices, swapped(): return lax.ppermute(array, 'space', swap)  18 us
    pallas_call x4, Pallas kernels, couple(): pl.pallas_call(functools.partial(couple_kernel, first, base, groups, grou...  14.9 us
    ppermute x15, waiting for transfers between devices, send(): lax.ppermute(after(parts[k], *events), 'sec', [(i, i ^ k) for i in range(...  13.1 us
    ppermute x15, starting transfers between devices, send(): lax.ppermute(after(parts[k], *events), 'sec', [(i, i ^ k) for i in range(...  9.4 us
    ppermute x3, starting transfers between devices, swapped(): return lax.ppermute(array, 'space', swap)  8.53 us
    ppermute x3, starting transfers between devices, hopped(): return lax.ppermute(array, 'space', pairs)  6.09 us
    pallas_call x1, Pallas kernels, sort(): pl.pallas_call(functools.partial(sort_kernel, outs, blocks), grid=(group_...  4 us
  transfers between devices with their start and end apart: 21, of which 9 were waited for; matrix products, arithmetic and copies ran while one was open for 0% of the time, Pallas kernels for 35%

profile of v2, /device:TPU:0, one launch (start us, length us, event | category | flops | bytes accessed | tf_op | source)
XLA Modules:
  0.0 98.3 jit_solution(13039444868756205854)
XLA Ops:
  0.6 0.1 pad_add_fusion.place_ref.refs_0_
  0.7 0.9 select_bitcast_fusion.refs_3_
  1.6 0.0 copy-start.1
  1.6 0.6 copy-done.1
  2.3 2.2 %select_upwind_rows.1 = (f32[18,64,128]{2,1,0:T(8,128)S(1)}, f32[16,128,128]{2,1,0:T(8,128)S(1)}, f32[128,128]{1,0:T(8,128)S(1)}) custom-call(f32[16]{0:T(128)S(1)} %copy-done.1, f32[16,640,128]{2,1,0:T(8,128)} %bitcast.34, f32[16,640,128]{2,1,0:T(8,128)} %bitcast.35, f32[16,640,128]{2,1,0:T(8,128)} %bitcast.36, f32[128,128]{1,0:T(8,128)S(1)} %select_bitcast_fusion.refs_3_), custom_call_target="tpu_custom_call" | custom-call | flops 3932160 | bytes 3932160 | tf_op jit(solution)/shard_map/select_upwind_rows/pallas_call | solution.py:428
  4.5 1.3 %collective-permute-start = (f32[18,64,128]{2,1,0:T(8,128)S(1)}, f32[18,64,128]{2,1,0:T(8,128)S(1)}, u32[]{:S(2)}, u32[]{:S(2)}) collective-permute-start(f32[18,64,128]{2,1,0:T(8,128)S(1)} %get-tuple-element.68.own_ref), channel_id=1, source_target_pairs={{2,0},{4,2},{6,4},{1,3},{3,5},{5,7},{10,8},{12,10},{14,12},{9,11},... | collective-permute-start | bytes 1769480 | tf_op jit(solution)/shard_map/ppermute | solution.py:530
  5.8 5.3 %collective-permute-start.9 = (f32[16,128,128]{2,1,0:T(8,128)S(1)}, f32[16,128,128]{2,1,0:T(8,128)S(1)}, u32[]{:S(2)}, u32[]{:S(2)}) collective-permute-start(f32[16,128,128]{2,1,0:T(8,128)S(1)} %get-tuple-element.83), channel_id=1, source_target_pairs={{0,1},{1,0},{2,3},{3,2},{4,5},{5,4},{6,7},{7,6},{8,9},{9,8},{10,11... | collective-permute-start | bytes 3145736 | tf_op jit(solution)/shard_map/ppermute | solution.py:527
  11.0 4.0 %sort_cells.1 = (f32[16,128,128]{2,1,0:T(8,128)S(1)}, f32[16,128,128]{2,1,0:T(8,128)S(1)}, f32[16,128,128]{2,1,0:T(8,128)S(1)}, f32[16,128,128]{2,1,0:T(8,128)S(...) custom-call(f32[16]{0:T(128)S(1)} %copy-done.2, f32[16,640,128]{2,1,0:T(8,128)} %bitcast.37), custom_call_target="tpu_custom_call" | custom-call | flops 6553600 | bytes 6553600 | tf_op jit(solution)/shard_map/sort_cells/pallas_call | solution.py:448
  15.0 1.3 %collective-permute-start.2 = (f32[16,128,128]{2,1,0:T(8,128)S(1)}, f32[16,128,128]{2,1,0:T(8,128)S(1)}, u32[]{:S(2)}, u32[]{:S(2)}) collective-permute-start(f32[16,128,128]{2,1,0:T(8,128)S(1)} %get-tuple-element.61._.own_ref), channel_id=1, source_target_pairs={{2,0},{4,2},{6,4},{1,3},{3,5},{5,7},{10,8},{12,10},{14,12},{9,11},... | collective-permute-start | bytes 3145736 | tf_op jit(solution)/shard_map/ppermute | solution.py:530
  16.3 6.3 %transport_inner_rows.1 = (f32[16,80,128]{2,1,0:T(8,128)S(1)}, f32[16,80,128]{2,1,0:T(8,128)S(1)}, f32[16,80,128]{2,1,0:T(8,128)S(1)}, f32[16,80,128]{2,1,0:T(8,128)S(1)}) custom-call(s32[2]{0:T(128)S(1)} %pad_add_fusion.place_ref.refs_0_, f32[16]{0:T(128)S(1)} %copy-done.2, f32[16]{0:T(128)S(1)} %copy-done.3, f32[5,16]{1,0:T(8,128)S(1)} %bitcast.27, ...), custom_call_target="tpu_custom_call" | custom-call | flops 6553600 | bytes 6553600 | tf_op jit(solution)/shard_map/transport_inner_rows/pallas_call | solution.py:468
  22.7 0.9 collective-permute-done.far_ref
  23.5 0.9 relay_upwind_rows.2._
  24.5 1.5 %collective-permute-start.1 = (f32[18,64,128]{2,1,0:T(8,128)S(1)}, f32[18,64,128]{2,1,0:T(8,128)S(1)}, u32[]{:S(2)}, u32[]{:S(2)}) collective-permute-start(f32[18,64,128]{2,1,0:T(8,128)S(1)} %relay_upwind_rows.2._), channel_id=1, source_target_pairs={{0,1},{1,0},{2,3},{3,2},{4,5},{5,4},{6,7},{7,6},{8,9},{9,8},{10,11... | collective-permute-start | bytes 1769480 | tf_op jit(solution)/shard_map/ppermute | solution.py:527
  26.0 0.1 collective-permute-start.3
  26.0 1.4 %collective-permute-start.4 = (f32[16,80,128]{2,1,0:T(8,128)S(1)}, f32[16,80,128]{2,1,0:T(8,128)S(1)}, u32[]{:S(2)}, u32[]{:S(2)}) collective-permute-start(f32[16,80,128]{2,1,0:T(8,128)S(1)} %get-tuple-element.75), channel_id=1, source_target_pairs={{0,16},{8,24},{16,0},{24,8},{1,17},{9,25},{17,1},{25,9},{2,18},{10... | collective-permute-start | bytes 1966088 | tf_op jit(solution)/shard_map/ppermute | solution.py:413
  27.5 7.6 %collective-permute-done.9.rest_2_.rest_4_ = f32[16,128,128]{2,1,0:T(8,128)S(1)} collective-permute-done((f32[16,128,128]{2,1,0:T(8,128)S(1)}, f32[16,128,128]{2,1,0:T(8,128)S(1)}, u32[]{:S(2)}, u32[]{:S(2)}) %collective-permute-start.9) | collective-permute-done | bytes 1048608 | tf_op jit(solution)/shard_map/ppermute | solution.py:527
  35.0 3.5 %collective-permute-start.10 = (f32[16,128,128]{2,1,0:T(8,128)S(1)}, f32[16,128,128]{2,1,0:T(8,128)S(1)}, u32[]{:S(2)}, u32[]{:S(2)}) collective-permute-start(f32[16,128,128]{2,1,0:T(8,128)S(1)} %collective-permute-done.9.rest_2_.rest_4_), channel_id=1, source_target_pairs={{0,2},{2,4},{4,6},{3,1},{5,3},{7,5},{8,10},{10,12},{12,14},{11,9},... | collective-permute-start | bytes 3145736 | tf_op jit(solution)/shard_map/ppermute | solution.py:530
  38.6 8.0 %collective-permute-done.1.edge_ref.rest_1_ = f32[18,64,128]{2,1,0:T(8,128)S(1)} collective-permute-done((f32[18,64,128]{2,1,0:T(8,128)S(1)}, f32[18,64,128]{2,1,0:T(8,128)S(1)}, u32[]{:S(2)}, u32[]{:S(2)}) %collective-permute-start.1) | collective-permute-done | bytes 589856 | tf_op jit(solution)/shard_map/ppermute | solution.py:527
  46.5 1.0 relay_upwind_rows.3._
  47.5 1.8 %collective-permute-start.12 = (f32[16,128,128]{2,1,0:T(8,128)S(1)}, f32[16,128,128]{2,1,0:T(8,128)S(1)}, u32[]{:S(2)}, u32[]{:S(2)}) collective-permute-start(f32[16,128,128]{2,1,0:T(8,128)S(1)} %relay_upwind_rows.3._), channel_id=1, source_target_pairs={{0,1},{1,0},{2,3},{3,2},{4,5},{5,4},{6,7},{7,6},{8,9},{9,8},{10,11... | collective-permute-start | bytes 3145736 | tf_op jit(solution)/shard_map/ppermute | solution.py:527
  49.4 2.3 %transport_outer_rows.4 = (f32[17,16,128]{2,1,0:T(8,128)S(1)}, f32[17,16,128]{2,1,0:T(8,128)S(1)}, f32[17,16,128]{2,1,0:T(8,128)S(1)}, f32[17,16,128]{2,1,0:T(8,128)S(1)}) custom-call(s32[2]{0:T(128)S(1)} %pad_add_fusion.place_ref.refs_0_, f32[16]{0:T(128)S(1)} %copy-done.2, f32[16]{0:T(128)S(1)} %copy-done.3, f32[5,16]{1,0:T(8,128)S(1)} %bitcast.30, ...), custom_call_target="tpu_custom_call" | custom-call | flops 1310720 | bytes 1310720 | tf_op jit(solution)/shard_map/transport_outer_rows/pallas_call | solution.py:468
  51.7 5.4 %collective-permute-done.4.refs_10_ = f32[16,80,128]{2,1,0:T(8,128)S(1)} collective-permute-done((f32[16,80,128]{2,1,0:T(8,128)S(1)}, f32[16,80,128]{2,1,0:T(8,128)S(1)}, u32[]{:S(2)}, u32[]{:S(2)}) %collective-permute-start.4) | collective-permute-done | bytes 655392 | tf_op jit(solution)/shard_map/ppermute | solution.py:413
  57.0 0.1 collective-permute-start.5
  57.1 0.7 collective-permute-start.7
  57.8 1.1 %collective-permute-start.8 = (f32[17,16,128]{2,1,0:T(8,128)S(1)}, f32[17,16,128]{2,1,0:T(8,128)S(1)}, u32[]{:S(2)}, u32[]{:S(2)}) collective-permute-start(f32[17,16,128]{2,1,0:T(8,128)S(1)} %get-tuple-element.81), channel_id=1, source_target_pairs={{0,24},{8,16},{16,8},{24,0},{1,25},{9,17},{17,9},{25,1},{2,26},{10... | collective-permute-start | bytes 417800 | tf_op jit(solution)/shard_map/ppermute | solution.py:413
  58.9 0.2 collective-permute-done.5.refs_9_
  59.1 0.1 collective-permute-start.6
  59.3 4.3 %collective-permute-done.7.refs_6_.refs_14_ = f32[17,16,128]{2,1,0:T(8,128)S(1)} collective-permute-done((f32[17,16,128]{2,1,0:T(8,128)S(1)}, f32[17,16,128]{2,1,0:T(8,128)S(1)}, u32[]{:S(2)}, u32[]{:S(2)}) %collective-permute-start.7) | collective-permute-done | bytes 139296 | tf_op jit(solution)/shard_map/ppermute | solution.py:413
  63.6 2.1 %collective-permute-done.8.refs_7_.refs_15_ = f32[17,16,128]{2,1,0:T(8,128)S(1)} collective-permute-done((f32[17,16,128]{2,1,0:T(8,128)S(1)}, f32[17,16,128]{2,1,0:T(8,128)S(1)}, u32[]{:S(2)}, u32[]{:S(2)}) %collective-permute-start.8) | collective-permute-done | bytes 139296 | tf_op jit(solution)/shard_map/ppermute | solution.py:413
  65.6 3.4 %transport_outer_rows.5 = (f32[16,32,128]{2,1,0:T(8,128)S(1)}, f32[16,32,128]{2,1,0:T(8,128)S(1)}, f32[16,32,128]{2,1,0:T(8,128)S(1)}, f32[16,32,128]{2,1,0:T(8,128)S(1)}) custom-call(s32[2]{0:T(128)S(1)} %pad_add_fusion.place_ref.refs_0_, f32[16]{0:T(128)S(1)} %copy-done.2, f32[16]{0:T(128)S(1)} %copy-done.3, f32[5,16]{1,0:T(8,128)S(1)} %bitcast.31, ...), custom_call_target="tpu_custom_call" | custom-call | flops 2621440 | bytes 2621440 | tf_op jit(solution)/shard_map/transport_outer_rows/pallas_call | solution.py:468
  69.1 0.1 collective-permute-start.11
  69.2 2.5 %collective-permute-done.12.rest_1_ = f32[16,128,128]{2,1,0:T(8,128)S(1)} collective-permute-done((f32[16,128,128]{2,1,0:T(8,128)S(1)}, f32[16,128,128]{2,1,0:T(8,128)S(1)}, u32[]{:S(2)}, u32[]{:S(2)}) %collective-permute-start.12) | collective-permute-done | bytes 1048608 | tf_op jit(solution)/shard_map/ppermute | solution.py:527
  71.7 1.7 %collective-permute-start.16 = (f32[16,32,128]{2,1,0:T(8,128)S(1)}, f32[16,32,128]{2,1,0:T(8,128)S(1)}, u32[]{:S(2)}, u32[]{:S(2)}) collective-permute-start(f32[16,32,128]{2,1,0:T(8,128)S(1)} %get-tuple-element.100), channel_id=1, source_target_pairs={{0,24},{8,16},{16,8},{24,0},{1,25},{9,17},{17,9},{25,1},{2,26},{10... | collective-permute-start | bytes 786440 | tf_op jit(solution)/shard_map/ppermute | solution.py:413
  73.3 0.1 pad_maximum_fusion.refs_2_
  73.4 0.1 pad_maximum_fusion.1.refs_16_
  73.5 3.6 %couple_sections.4 = (f32[64,160,128]{2,1,0:T(8,128)}, f32[5,8,512]{2,1,0:T(8,128)}, f32[8,64,512]{2,1,0:T(8,128)S(1)}) custom-call(s32[2]{0:T(128)S(1)} %pad_add_fusion.place_ref.refs_0_, f32[64]{0:T(128)S(1)} %copy-done.4, bf16[64,192]{1,0:T(8,128)(2,1)S(1)} %pad_maximum_fusion.refs_2_, f32[32,128]{1,0:T(8,128)S(1)} %bitcast.23, ...), custom_call_target="tpu_custom_call" | custom-call | flops 33554432 | bytes 3145728 | tf_op jit(solution)/shard_map/couple_sections/pallas_call | solution.py:567
  77.1 1.1 %collective-permute-done.11.refs_14_ = f32[16,32,128]{2,1,0:T(8,128)S(1)} collective-permute-done((f32[16,32,128]{2,1,0:T(8,128)S(1)}, f32[16,32,128]{2,1,0:T(8,128)S(1)}, u32[]{:S(2)}, u32[]{:S(2)}) %collective-permute-start.11) | collective-permute-done | bytes 262176 | tf_op jit(solution)/shard_map/ppermute | solution.py:413
  78.2 2.3 %transport_outer_rows.6 = (f32[16,16,128]{2,1,0:T(8,128)S(1)}, f32[16,16,128]{2,1,0:T(8,128)S(1)}, f32[16,16,128]{2,1,0:T(8,128)S(1)}, f32[16,16,128]{2,1,0:T(8,128)S(1)}) custom-call(s32[2]{0:T(128)S(1)} %pad_add_fusion.place_ref.refs_0_, f32[16]{0:T(128)S(1)} %copy-done.2, f32[16]{0:T(128)S(1)} %copy-done.3, f32[5,16]{1,0:T(8,128)S(1)} %bitcast.32, ...), custom_call_target="tpu_custom_call" | custom-call | flops 1310720 | bytes 1310720 | tf_op jit(solution)/shard_map/transport_outer_rows/pallas_call | solution.py:468
  80.5 0.1 collective-permute-start.14
  80.6 0.2 collective-permute-start.19
  80.8 1.7 %collective-permute-start.20 = (f32[16,16,128]{2,1,0:T(8,128)S(1)}, f32[16,16,128]{2,1,0:T(8,128)S(1)}, u32[]{:S(2)}, u32[]{:S(2)}) collective-permute-start(f32[16,16,128]{2,1,0:T(8,128)S(1)} %get-tuple-element.105), channel_id=1, source_target_pairs={{0,24},{8,16},{16,8},{24,0},{1,25},{9,17},{17,9},{25,1},{2,26},{10... | collective-permute-start | bytes 393224 | tf_op jit(solution)/shard_map/ppermute | solution.py:413
  82.5 2.3 %transport_outer_rows.7 = (f32[16,16,128]{2,1,0:T(8,128)S(1)}, f32[16,16,128]{2,1,0:T(8,128)S(1)}, f32[16,16,128]{2,1,0:T(8,128)S(1)}, f32[16,16,128]{2,1,0:T(8,128)S(1)}) custom-call(s32[2]{0:T(128)S(1)} %pad_add_fusion.place_ref.refs_0_, f32[16]{0:T(128)S(1)} %copy-done.2, f32[16]{0:T(128)S(1)} %copy-done.3, f32[5,16]{1,0:T(8,128)S(1)} %bitcast.33, ...), custom_call_target="tpu_custom_call" | custom-call | flops 1310720 | bytes 1310720 | tf_op jit(solution)/shard_map/transport_outer_rows/pallas_call | solution.py:468
  84.8 0.4 collective-permute-start.17
  85.1 1.4 %collective-permute-start.18 = (f32[16,16,128]{2,1,0:T(8,128)S(1)}, f32[16,16,128]{2,1,0:T(8,128)S(1)}, u32[]{:S(2)}, u32[]{:S(2)}) collective-permute-start(f32[16,16,128]{2,1,0:T(8,128)S(1)} %get-tuple-element.103), channel_id=1, source_target_pairs={{0,24},{8,16},{16,8},{24,0},{1,25},{9,17},{17,9},{25,1},{2,26},{10... | collective-permute-start | bytes 393224 | tf_op jit(solution)/shard_map/ppermute | solution.py:413
  86.5 0.4 collective-permute-start.15
  87.0 4.9 %couple_sections.5 = (f32[64,160,128]{2,1,0:T(8,128)}, f32[5,8,512]{2,1,0:T(8,128)}) custom-call(s32[2]{0:T(128)S(1)} %pad_add_fusion.place_ref.refs_0_, f32[64]{0:T(128)S(1)} %copy-done.4, bf16[64,192]{1,0:T(8,128)(2,1)S(1)} %pad_maximum_fusion.refs_2_, f32[32,128]{1,0:T(8,128)S(1)} %bitcast.24, ...), custom_call_target="tpu_custom_call", output_to_operand_aliasing={{0}: (17, {}), {1}: (18, {})} | custom-call | flops 67108864 | bytes 6291456 | tf_op jit(solution)/shard_map/couple_sections/pallas_call | solution.py:567
  91.9 3.2 %couple_sections.6 = (f32[64,160,128]{2,1,0:T(8,128)}, f32[5,8,512]{2,1,0:T(8,128)}) custom-call(s32[2]{0:T(128)S(1)} %pad_add_fusion.place_ref.refs_0_, f32[64]{0:T(128)S(1)} %copy-done.4, bf16[64,192]{1,0:T(8,128)(2,1)S(1)} %pad_maximum_fusion.refs_2_, f32[32,128]{1,0:T(8,128)S(1)} %bitcast.25, ...), custom_call_target="tpu_custom_call", output_to_operand_aliasing={{0}: (17, {}), {1}: (18, {})} | custom-call | flops 33554432 | bytes 3145728 | tf_op jit(solution)/shard_map/couple_sections/pallas_call | solution.py:567
  95.1 3.2 %couple_sections.7 = (f32[64,160,128]{2,1,0:T(8,128)}, f32[5,8,512]{2,1,0:T(8,128)}) custom-call(s32[2]{0:T(128)S(1)} %pad_add_fusion.place_ref.refs_0_, f32[64]{0:T(128)S(1)} %copy-done.4, bf16[64,192]{1,0:T(8,128)(2,1)S(1)} %pad_maximum_fusion.refs_2_, f32[32,128]{1,0:T(8,128)S(1)} %bitcast.26, ...), custom_call_target="tpu_custom_call", output_to_operand_aliasing={{0}: (17, {}), {1}: (18, {})} | custom-call | flops 33554432 | bytes 3145728 | tf_op jit(solution)/shard_map/couple_sections/pallas_call | solution.py:567
  (30 shorter events, 0.1 us)
Async XLA Ops:
  1.6 0.7 copy-start.1
  2.3 8.8 %copy-start.2 = (f32[16]{0:T(128)S(1)}, f32[16]{0:T(128)}, u32[]{:S(2)}) copy-start(f32[16]{0:T(128)} %ux_ref.15) | copy-start | bytes 196
  4.4 11.9 %copy-start = (f32[16,5]{0,1:T(8,128)S(1)}, f32[16,5]{0,1:T(8,128)}, u32[]{:S(2)}) copy-start(f32[16,5]{0,1:T(8,128)} %param.13) | copy-start | bytes 964
  4.5 11.9 %copy-start.3 = (f32[16]{0:T(128)S(1)}, f32[16]{0:T(128)}, u32[]{:S(2)}) copy-start(f32[16]{0:T(128)} %uy_ref.13) | copy-start | bytes 196
  4.5 19.1 %collective-permute-start = (f32[18,64,128]{2,1,0:T(8,128)S(1)}, f32[18,64,128]{2,1,0:T(8,128)S(1)}, u32[]{:S(2)}, u32[]{:S(2)}) collective-permute-start(f32[18,64,128]{2,1,0:T(8,128)S(1)} %get-tuple-element.68.own_ref), channel_id=1, source_target_pairs={{2,0},{4,2},{6,4},{1,3},{3,5},{5,7},{10,8},{12,10},{14,12},{9,11},... | collective-permute-start | bytes 1769480 | tf_op jit(solution)/shard_map/ppermute | solution.py:530
  5.8 29.3 %collective-permute-start.9 = (f32[16,128,128]{2,1,0:T(8,128)S(1)}, f32[16,128,128]{2,1,0:T(8,128)S(1)}, u32[]{:S(2)}, u32[]{:S(2)}) collective-permute-start(f32[16,128,128]{2,1,0:T(8,128)S(1)} %get-tuple-element.83), channel_id=1, source_target_pairs={{0,1},{1,0},{2,3},{3,2},{4,5},{5,4},{6,7},{7,6},{8,9},{9,8},{10,11... | collective-permute-start | bytes 3145736 | tf_op jit(solution)/shard_map/ppermute | solution.py:527
  15.0 31.5 %collective-permute-start.2 = (f32[16,128,128]{2,1,0:T(8,128)S(1)}, f32[16,128,128]{2,1,0:T(8,128)S(1)}, u32[]{:S(2)}, u32[]{:S(2)}) collective-permute-start(f32[16,128,128]{2,1,0:T(8,128)S(1)} %get-tuple-element.61._.own_ref), channel_id=1, source_target_pairs={{2,0},{4,2},{6,4},{1,3},{3,5},{5,7},{10,8},{12,10},{14,12},{9,11},... | collective-permute-start | bytes 3145736 | tf_op jit(solution)/shard_map/ppermute | solution.py:530
  22.7 36.6 %copy-start.5 = (f32[64,64]{1,0:T(8,128)S(1)}, f32[64,64]{1,0:T(8,128)}, u32[]{:S(2)}) copy-start(f32[64,64]{1,0:T(8,128)} %param.17) | copy-start | bytes 49156
  24.5 22.0 %collective-permute-start.1 = (f32[18,64,128]{2,1,0:T(8,128)S(1)}, f32[18,64,128]{2,1,0:T(8,128)S(1)}, u32[]{:S(2)}, u32[]{:S(2)}) collective-permute-start(f32[18,64,128]{2,1,0:T(8,128)S(1)} %relay_upwind_rows.2._), channel_id=1, source_target_pairs={{0,1},{1,0},{2,3},{3,2},{4,5},{5,4},{6,7},{7,6},{8,9},{9,8},{10,11... | collective-permute-start | bytes 1769480 | tf_op jit(solution)/shard_map/ppermute | solution.py:527
  26.0 23.4 %collective-permute-start.3 = (f32[16,80,128]{2,1,0:T(8,128)S(1)}, f32[16,80,128]{2,1,0:T(8,128)S(1)}, u32[]{:S(2)}, u32[]{:S(2)}) collective-permute-start(f32[16,80,128]{2,1,0:T(8,128)S(1)} %get-tuple-element.70), channel_id=1, source_target_pairs={{0,24},{8,16},{16,8},{24,0},{1,25},{9,17},{17,9},{25,1},{2,26},{10... | collective-permute-start | bytes 1966088 | tf_op jit(solution)/shard_map/ppermute | solution.py:413
  26.0 31.0 %collective-permute-start.4 = (f32[16,80,128]{2,1,0:T(8,128)S(1)}, f32[16,80,128]{2,1,0:T(8,128)S(1)}, u32[]{:S(2)}, u32[]{:S(2)}) collective-permute-start(f32[16,80,128]{2,1,0:T(8,128)S(1)} %get-tuple-element.75), channel_id=1, source_target_pairs={{0,16},{8,24},{16,0},{24,8},{1,17},{9,25},{17,1},{25,9},{2,18},{10... | collective-permute-start | bytes 1966088 | tf_op jit(solution)/shard_map/ppermute | solution.py:413
  35.0 30.6 %collective-permute-start.10 = (f32[16,128,128]{2,1,0:T(8,128)S(1)}, f32[16,128,128]{2,1,0:T(8,128)S(1)}, u32[]{:S(2)}, u32[]{:S(2)}) collective-permute-start(f32[16,128,128]{2,1,0:T(8,128)S(1)} %collective-permute-done.9.rest_2_.rest_4_), channel_id=1, source_target_pairs={{0,2},{2,4},{4,6},{3,1},{5,3},{7,5},{8,10},{10,12},{12,14},{11,9},... | collective-permute-start | bytes 3145736 | tf_op jit(solution)/shard_map/ppermute | solution.py:530
  47.5 24.1 %copy-start.6 = (f32[64,64]{1,0:T(8,128)S(1)}, f32[64,64]{1,0:T(8,128)}, u32[]{:S(2)}) copy-start(f32[64,64]{1,0:T(8,128)} %param.16) | copy-start | bytes 49156
  47.5 25.9 %copy-start.7 = (f32[8,512]{1,0:T(8,128)S(1)}, f32[8,512]{1,0:T(8,128)}, u32[]{:S(2)}) copy-start(f32[8,512]{1,0:T(8,128)} %param.19) | copy-start | bytes 49156
  47.5 26.0 %copy-start.4 = (f32[64]{0:T(128)S(1)}, f32[64]{0:T(128)}, u32[]{:S(2)}) copy-start(f32[64]{0:T(128)} %refs_1_.7) | copy-start | bytes 772
  47.5 24.1 %collective-permute-start.12 = (f32[16,128,128]{2,1,0:T(8,128)S(1)}, f32[16,128,128]{2,1,0:T(8,128)S(1)}, u32[]{:S(2)}, u32[]{:S(2)}) collective-permute-start(f32[16,128,128]{2,1,0:T(8,128)S(1)} %relay_upwind_rows.3._), channel_id=1, source_target_pairs={{0,1},{1,0},{2,3},{3,2},{4,5},{5,4},{6,7},{7,6},{8,9},{9,8},{10,11... | collective-permute-start | bytes 3145736 | tf_op jit(solution)/shard_map/ppermute | solution.py:527
  57.0 2.1 %collective-permute-start.5 = (f32[16,80,128]{2,1,0:T(8,128)S(1)}, f32[16,80,128]{2,1,0:T(8,128)S(1)}, u32[]{:S(2)}, u32[]{:S(2)}) collective-permute-start(f32[16,80,128]{2,1,0:T(8,128)S(1)} %get-tuple-element.76), channel_id=1, source_target_pairs={{0,8},{8,0},{16,24},{24,16},{1,9},{9,1},{17,25},{25,17},{2,10},{10... | collective-permute-start | bytes 1966088 | tf_op jit(solution)/shard_map/ppermute | solution.py:413
  57.1 6.5 %collective-permute-start.7 = (f32[17,16,128]{2,1,0:T(8,128)S(1)}, f32[17,16,128]{2,1,0:T(8,128)S(1)}, u32[]{:S(2)}, u32[]{:S(2)}) collective-permute-start(f32[17,16,128]{2,1,0:T(8,128)S(1)} %get-tuple-element.79), channel_id=1, source_target_pairs={{0,16},{8,24},{16,0},{24,8},{1,17},{9,25},{17,1},{25,9},{2,18},{10... | collective-permute-start | bytes 417800 | tf_op jit(solution)/shard_map/ppermute | solution.py:413
  57.8 7.8 %collective-permute-start.8 = (f32[17,16,128]{2,1,0:T(8,128)S(1)}, f32[17,16,128]{2,1,0:T(8,128)S(1)}, u32[]{:S(2)}, u32[]{:S(2)}) collective-permute-start(f32[17,16,128]{2,1,0:T(8,128)S(1)} %get-tuple-element.81), channel_id=1, source_target_pairs={{0,24},{8,16},{16,8},{24,0},{1,25},{9,17},{17,9},{25,1},{2,26},{10... | collective-permute-start | bytes 417800 | tf_op jit(solution)/shard_map/ppermute | solution.py:413
  59.1 10.0 %collective-permute-start.6 = (f32[17,16,128]{2,1,0:T(8,128)S(1)}, f32[17,16,128]{2,1,0:T(8,128)S(1)}, u32[]{:S(2)}, u32[]{:S(2)}) collective-permute-start(f32[17,16,128]{2,1,0:T(8,128)S(1)} %get-tuple-element.77), channel_id=1, source_target_pairs={{0,8},{8,0},{16,24},{24,16},{1,9},{9,1},{17,25},{25,17},{2,10},{10... | collective-permute-start | bytes 417800 | tf_op jit(solution)/shard_map/ppermute | solution.py:413
  69.1 9.2 %collective-permute-start.11 = (f32[16,32,128]{2,1,0:T(8,128)S(1)}, f32[16,32,128]{2,1,0:T(8,128)S(1)}, u32[]{:S(2)}, u32[]{:S(2)}) collective-permute-start(f32[16,32,128]{2,1,0:T(8,128)S(1)} %get-tuple-element.88), channel_id=1, source_target_pairs={{0,16},{8,24},{16,0},{24,8},{1,17},{9,25},{17,1},{25,9},{2,18},{10... | collective-permute-start | bytes 786440 | tf_op jit(solution)/shard_map/ppermute | solution.py:413
  71.6 8.9 %collective-permute-start.13 = (f32[16,32,128]{2,1,0:T(8,128)S(1)}, f32[16,32,128]{2,1,0:T(8,128)S(1)}, u32[]{:S(2)}, u32[]{:S(2)}) collective-permute-start(f32[16,32,128]{2,1,0:T(8,128)S(1)} %get-tuple-element.95), channel_id=1, source_target_pairs={{0,8},{8,0},{16,24},{24,16},{1,9},{9,1},{17,25},{25,17},{2,10},{10... | collective-permute-start | bytes 786440 | tf_op jit(solution)/shard_map/ppermute | solution.py:413
  71.7 13.1 %collective-permute-start.16 = (f32[16,32,128]{2,1,0:T(8,128)S(1)}, f32[16,32,128]{2,1,0:T(8,128)S(1)}, u32[]{:S(2)}, u32[]{:S(2)}) collective-permute-start(f32[16,32,128]{2,1,0:T(8,128)S(1)} %get-tuple-element.100), channel_id=1, source_target_pairs={{0,24},{8,16},{16,8},{24,0},{1,25},{9,17},{17,9},{25,1},{2,26},{10... | collective-permute-start | bytes 786440 | tf_op jit(solution)/shard_map/ppermute | solution.py:413
  80.5 6.0 %collective-permute-start.14 = (f32[16,16,128]{2,1,0:T(8,128)S(1)}, f32[16,16,128]{2,1,0:T(8,128)S(1)}, u32[]{:S(2)}, u32[]{:S(2)}) collective-permute-start(f32[16,16,128]{2,1,0:T(8,128)S(1)} %get-tuple-element.96), channel_id=1, source_target_pairs={{0,8},{8,0},{16,24},{24,16},{1,9},{9,1},{17,25},{25,17},{2,10},{10... | collective-permute-start | bytes 393224 | tf_op jit(solution)/shard_map/ppermute | solution.py:413
  80.6 11.3 %collective-permute-start.19 = (f32[16,16,128]{2,1,0:T(8,128)S(1)}, f32[16,16,128]{2,1,0:T(8,128)S(1)}, u32[]{:S(2)}, u32[]{:S(2)}) collective-permute-start(f32[16,16,128]{2,1,0:T(8,128)S(1)} %get-tuple-element.104), channel_id=1, source_target_pairs={{0,16},{8,24},{16,0},{24,8},{1,17},{9,25},{17,1},{25,9},{2,18},{10... | collective-permute-start | bytes 393224 | tf_op jit(solution)/shard_map/ppermute | solution.py:413
  80.8 11.1 %collective-permute-start.20 = (f32[16,16,128]{2,1,0:T(8,128)S(1)}, f32[16,16,128]{2,1,0:T(8,128)S(1)}, u32[]{:S(2)}, u32[]{:S(2)}) collective-permute-start(f32[16,16,128]{2,1,0:T(8,128)S(1)} %get-tuple-element.105), channel_id=1, source_target_pairs={{0,24},{8,16},{16,8},{24,0},{1,25},{9,17},{17,9},{25,1},{2,26},{10... | collective-permute-start | bytes 393224 | tf_op jit(solution)/shard_map/ppermute | solution.py:413
  84.8 10.3 %collective-permute-start.17 = (f32[16,16,128]{2,1,0:T(8,128)S(1)}, f32[16,16,128]{2,1,0:T(8,128)S(1)}, u32[]{:S(2)}, u32[]{:S(2)}) collective-permute-start(f32[16,16,128]{2,1,0:T(8,128)S(1)} %get-tuple-element.101), channel_id=1, source_target_pairs={{0,16},{8,24},{16,0},{24,8},{1,17},{9,25},{17,1},{25,9},{2,18},{10... | collective-permute-start | bytes 393224 | tf_op jit(solution)/shard_map/ppermute | solution.py:413
  85.1 10.0 %collective-permute-start.18 = (f32[16,16,128]{2,1,0:T(8,128)S(1)}, f32[16,16,128]{2,1,0:T(8,128)S(1)}, u32[]{:S(2)}, u32[]{:S(2)}) collective-permute-start(f32[16,16,128]{2,1,0:T(8,128)S(1)} %get-tuple-element.103), channel_id=1, source_target_pairs={{0,24},{8,16},{16,8},{24,0},{1,25},{9,17},{17,9},{25,1},{2,26},{10... | collective-permute-start | bytes 393224 | tf_op jit(solution)/shard_map/ppermute | solution.py:413
  86.5 8.6 %collective-permute-start.15 = (f32[16,16,128]{2,1,0:T(8,128)S(1)}, f32[16,16,128]{2,1,0:T(8,128)S(1)}, u32[]{:S(2)}, u32[]{:S(2)}) collective-permute-start(f32[16,16,128]{2,1,0:T(8,128)S(1)} %get-tuple-element.97), channel_id=1, source_target_pairs={{0,8},{8,0},{16,24},{24,16},{1,9},{9,1},{17,25},{25,17},{2,10},{10... | collective-permute-start | bytes 393224 | tf_op jit(solution)/shard_map/ppermute | solution.py:413

commit v3 on v2

--- a/solution.py
+++ b/solution.py
@@ -343,7 +343,7 @@
                 rest[pl.ds(i * half * sections + number, half, stride=sections), :] = moved - evaporated
             return tuple(result)
 
-        gas = lax.fori_loop(0, group_size, section, gas, unroll=4)
+        gas = lax.fori_loop(0, group_size, section, gas, unroll=16)
     for i in range(2):
         total[i * half : (i + 1) * half, :] = gas[i]
     for block in range(blocks):

time: 98.6 us -> 98.3 us (level)
  no operation moved by 1% of the time
where the time goes in v3:
time: 98.3 us; the launch traced here: 98 us
  Pallas kernels  39.1 us (40%)
  waiting for transfers between devices  32.1 us (33%)
  starting transfers between devices  24 us (24%)
  other arithmetic  1.14 us (1%)
    pallas_call x7, Pallas kernels, whole(): pl.pallas_call(kernel, in_specs=[smem] * 4 + [anywhere] + [vmem] * len(op...  18.5 us
    ppermute x3, waiting for transfers between devices, swapped(): return lax.ppermute(array, 'space', swap)  18 us
    pallas_call x4, Pallas kernels, couple(): pl.pallas_call(functools.partial(couple_kernel, first, base, groups, grou...  14.4 us
    ppermute x15, waiting for transfers between devices, send(): lax.ppermute(after(parts[k], *events), 'sec', [(i, i ^ k) for i in range(...  13.2 us
    ppermute x15, starting transfers between devices, send(): lax.ppermute(after(parts[k], *events), 'sec', [(i, i ^ k) for i in range(...  9.4 us
    ppermute x3, starting transfers between devices, swapped(): return lax.ppermute(array, 'space', swap)  8.53 us
    ppermute x3, starting transfers between devices, hopped(): return lax.ppermute(array, 'space', pairs)  6.09 us
    pallas_call x1, Pallas kernels, sort(): pl.pallas_call(functools.partial(sort_kernel, outs, blocks), grid=(group_...  4 us
  transfers between devices with their start and end apart: 21, of which 9 were waited for; matrix products, arithmetic and copies ran while one was open for 0% of the time, Pallas kernels for 35%

profile of v3, /device:TPU:0, one launch (start us, length us, event | category | flops | bytes accessed | tf_op | source)
XLA Modules:
  0.0 98.0 jit_solution(2529110974811895673)
XLA Ops:
  0.6 0.1 pad_add_fusion.place_ref.refs_0_
  0.7 0.9 select_bitcast_fusion.refs_3_
  1.6 0.0 copy-start.1
  1.6 0.6 copy-done.1
  2.3 2.2 %select_upwind_rows.1 = (f32[18,64,128]{2,1,0:T(8,128)S(1)}, f32[16,128,128]{2,1,0:T(8,128)S(1)}, f32[128,128]{1,0:T(8,128)S(1)}) custom-call(f32[16]{0:T(128)S(1)} %copy-done.1, f32[16,640,128]{2,1,0:T(8,128)} %bitcast.34, f32[16,640,128]{2,1,0:T(8,128)} %bitcast.35, f32[16,640,128]{2,1,0:T(8,128)} %bitcast.36, f32[128,128]{1,0:T(8,128)S(1)} %select_bitcast_fusion.refs_3_), custom_call_target="tpu_custom_call" | custom-call | flops 3932160 | bytes 3932160 | tf_op jit(solution)/shard_map/select_upwind_rows/pallas_call | solution.py:428
  4.5 1.3 %collective-permute-start = (f32[18,64,128]{2,1,0:T(8,128)S(1)}, f32[18,64,128]{2,1,0:T(8,128)S(1)}, u32[]{:S(2)}, u32[]{:S(2)}) collective-permute-start(f32[18,64,128]{2,1,0:T(8,128)S(1)} %get-tuple-element.68.own_ref), channel_id=1, source_target_pairs={{2,0},{4,2},{6,4},{1,3},{3,5},{5,7},{10,8},{12,10},{14,12},{9,11},... | collective-permute-start | bytes 1769480 | tf_op jit(solution)/shard_map/ppermute | solution.py:530
  5.8 5.3 %collective-permute-start.9 = (f32[16,128,128]{2,1,0:T(8,128)S(1)}, f32[16,128,128]{2,1,0:T(8,128)S(1)}, u32[]{:S(2)}, u32[]{:S(2)}) collective-permute-start(f32[16,128,128]{2,1,0:T(8,128)S(1)} %get-tuple-element.83), channel_id=1, source_target_pairs={{0,1},{1,0},{2,3},{3,2},{4,5},{5,4},{6,7},{7,6},{8,9},{9,8},{10,11... | collective-permute-start | bytes 3145736 | tf_op jit(solution)/shard_map/ppermute | solution.py:527
  11.0 4.0 %sort_cells.1 = (f32[16,128,128]{2,1,0:T(8,128)S(1)}, f32[16,128,128]{2,1,0:T(8,128)S(1)}, f32[16,128,128]{2,1,0:T(8,128)S(1)}, f32[16,128,128]{2,1,0:T(8,128)S(...) custom-call(f32[16]{0:T(128)S(1)} %copy-done.2, f32[16,640,128]{2,1,0:T(8,128)} %bitcast.37), custom_call_target="tpu_custom_call" | custom-call | flops 6553600 | bytes 6553600 | tf_op jit(solution)/shard_map/sort_cells/pallas_call | solution.py:448
  15.0 1.3 %collective-permute-start.2 = (f32[16,128,128]{2,1,0:T(8,128)S(1)}, f32[16,128,128]{2,1,0:T(8,128)S(1)}, u32[]{:S(2)}, u32[]{:S(2)}) collective-permute-start(f32[16,128,128]{2,1,0:T(8,128)S(1)} %get-tuple-element.61._.own_ref), channel_id=1, source_target_pairs={{2,0},{4,2},{6,4},{1,3},{3,5},{5,7},{10,8},{12,10},{14,12},{9,11},... | collective-permute-start | bytes 3145736 | tf_op jit(solution)/shard_map/ppermute | solution.py:530
  16.3 6.3 %transport_inner_rows.1 = (f32[16,80,128]{2,1,0:T(8,128)S(1)}, f32[16,80,128]{2,1,0:T(8,128)S(1)}, f32[16,80,128]{2,1,0:T(8,128)S(1)}, f32[16,80,128]{2,1,0:T(8,128)S(1)}) custom-call(s32[2]{0:T(128)S(1)} %pad_add_fusion.place_ref.refs_0_, f32[16]{0:T(128)S(1)} %copy-done.2, f32[16]{0:T(128)S(1)} %copy-done.3, f32[5,16]{1,0:T(8,128)S(1)} %bitcast.27, ...), custom_call_target="tpu_custom_call" | custom-call | flops 6553600 | bytes 6553600 | tf_op jit(solution)/shard_map/transport_inner_rows/pallas_call | solution.py:468
  22.7 0.9 collective-permute-done.far_ref
  23.5 0.9 relay_upwind_rows.2._
  24.5 1.5 %collective-permute-start.1 = (f32[18,64,128]{2,1,0:T(8,128)S(1)}, f32[18,64,128]{2,1,0:T(8,128)S(1)}, u32[]{:S(2)}, u32[]{:S(2)}) collective-permute-start(f32[18,64,128]{2,1,0:T(8,128)S(1)} %relay_upwind_rows.2._), channel_id=1, source_target_pairs={{0,1},{1,0},{2,3},{3,2},{4,5},{5,4},{6,7},{7,6},{8,9},{9,8},{10,11... | collective-permute-start | bytes 1769480 | tf_op jit(solution)/shard_map/ppermute | solution.py:527
  26.0 0.1 collective-permute-start.3
  26.1 1.4 %collective-permute-start.4 = (f32[16,80,128]{2,1,0:T(8,128)S(1)}, f32[16,80,128]{2,1,0:T(8,128)S(1)}, u32[]{:S(2)}, u32[]{:S(2)}) collective-permute-start(f32[16,80,128]{2,1,0:T(8,128)S(1)} %get-tuple-element.75), channel_id=1, source_target_pairs={{0,16},{8,24},{16,0},{24,8},{1,17},{9,25},{17,1},{25,9},{2,18},{10... | collective-permute-start | bytes 1966088 | tf_op jit(solution)/shard_map/ppermute | solution.py:413
  27.5 7.6 %collective-permute-done.9.rest_2_.rest_4_ = f32[16,128,128]{2,1,0:T(8,128)S(1)} collective-permute-done((f32[16,128,128]{2,1,0:T(8,128)S(1)}, f32[16,128,128]{2,1,0:T(8,128)S(1)}, u32[]{:S(2)}, u32[]{:S(2)}) %collective-permute-start.9) | collective-permute-done | bytes 1048608 | tf_op jit(solution)/shard_map/ppermute | solution.py:527
  35.0 3.5 %collective-permute-start.10 = (f32[16,128,128]{2,1,0:T(8,128)S(1)}, f32[16,128,128]{2,1,0:T(8,128)S(1)}, u32[]{:S(2)}, u32[]{:S(2)}) collective-permute-start(f32[16,128,128]{2,1,0:T(8,128)S(1)} %collective-permute-done.9.rest_2_.rest_4_), channel_id=1, source_target_pairs={{0,2},{2,4},{4,6},{3,1},{5,3},{7,5},{8,10},{10,12},{12,14},{11,9},... | collective-permute-start | bytes 3145736 | tf_op jit(solution)/shard_map/ppermute | solution.py:530
  38.6 8.0 %collective-permute-done.1.edge_ref.rest_1_ = f32[18,64,128]{2,1,0:T(8,128)S(1)} collective-permute-done((f32[18,64,128]{2,1,0:T(8,128)S(1)}, f32[18,64,128]{2,1,0:T(8,128)S(1)}, u32[]{:S(2)}, u32[]{:S(2)}) %collective-permute-start.1) | collective-permute-done | bytes 589856 | tf_op jit(solution)/shard_map/ppermute | solution.py:527
  46.5 1.0 relay_upwind_rows.3._
  47.5 1.8 %collective-permute-start.12 = (f32[16,128,128]{2,1,0:T(8,128)S(1)}, f32[16,128,128]{2,1,0:T(8,128)S(1)}, u32[]{:S(2)}, u32[]{:S(2)}) collective-permute-start(f32[16,128,128]{2,1,0:T(8,128)S(1)} %relay_upwind_rows.3._), channel_id=1, source_target_pairs={{0,1},{1,0},{2,3},{3,2},{4,5},{5,4},{6,7},{7,6},{8,9},{9,8},{10,11... | collective-permute-start | bytes 3145736 | tf_op jit(solution)/shard_map/ppermute | solution.py:527
  49.4 2.3 %transport_outer_rows.4 = (f32[17,16,128]{2,1,0:T(8,128)S(1)}, f32[17,16,128]{2,1,0:T(8,128)S(1)}, f32[17,16,128]{2,1,0:T(8,128)S(1)}, f32[17,16,128]{2,1,0:T(8,128)S(1)}) custom-call(s32[2]{0:T(128)S(1)} %pad_add_fusion.place_ref.refs_0_, f32[16]{0:T(128)S(1)} %copy-done.2, f32[16]{0:T(128)S(1)} %copy-done.3, f32[5,16]{1,0:T(8,128)S(1)} %bitcast.30, ...), custom_call_target="tpu_custom_call" | custom-call | flops 1310720 | bytes 1310720 | tf_op jit(solution)/shard_map/transport_outer_rows/pallas_call | solution.py:468
  51.7 5.4 %collective-permute-done.4.refs_10_ = f32[16,80,128]{2,1,0:T(8,128)S(1)} collective-permute-done((f32[16,80,128]{2,1,0:T(8,128)S(1)}, f32[16,80,128]{2,1,0:T(8,128)S(1)}, u32[]{:S(2)}, u32[]{:S(2)}) %collective-permute-start.4) | collective-permute-done | bytes 655392 | tf_op jit(solution)/shard_map/ppermute | solution.py:413
  57.0 0.1 collective-permute-start.5
  57.1 0.7 collective-permute-start.7
  57.8 1.1 %collective-permute-start.8 = (f32[17,16,128]{2,1,0:T(8,128)S(1)}, f32[17,16,128]{2,1,0:T(8,128)S(1)}, u32[]{:S(2)}, u32[]{:S(2)}) collective-permute-start(f32[17,16,128]{2,1,0:T(8,128)S(1)} %get-tuple-element.81), channel_id=1, source_target_pairs={{0,24},{8,16},{16,8},{24,0},{1,25},{9,17},{17,9},{25,1},{2,26},{10... | collective-permute-start | bytes 417800 | tf_op jit(solution)/shard_map/ppermute | solution.py:413
  58.9 0.2 collective-permute-done.5.refs_9_
  59.1 0.1 collective-permute-start.6
  59.3 4.3 %collective-permute-done.7.refs_6_.refs_14_ = f32[17,16,128]{2,1,0:T(8,128)S(1)} collective-permute-done((f32[17,16,128]{2,1,0:T(8,128)S(1)}, f32[17,16,128]{2,1,0:T(8,128)S(1)}, u32[]{:S(2)}, u32[]{:S(2)}) %collective-permute-start.7) | collective-permute-done | bytes 139296 | tf_op jit(solution)/shard_map/ppermute | solution.py:413
  63.6 2.1 %collective-permute-done.8.refs_7_.refs_15_ = f32[17,16,128]{2,1,0:T(8,128)S(1)} collective-permute-done((f32[17,16,128]{2,1,0:T(8,128)S(1)}, f32[17,16,128]{2,1,0:T(8,128)S(1)}, u32[]{:S(2)}, u32[]{:S(2)}) %collective-permute-start.8) | collective-permute-done | bytes 139296 | tf_op jit(solution)/shard_map/ppermute | solution.py:413
  65.7 3.4 %transport_outer_rows.5 = (f32[16,32,128]{2,1,0:T(8,128)S(1)}, f32[16,32,128]{2,1,0:T(8,128)S(1)}, f32[16,32,128]{2,1,0:T(8,128)S(1)}, f32[16,32,128]{2,1,0:T(8,128)S(1)}) custom-call(s32[2]{0:T(128)S(1)} %pad_add_fusion.place_ref.refs_0_, f32[16]{0:T(128)S(1)} %copy-done.2, f32[16]{0:T(128)S(1)} %copy-done.3, f32[5,16]{1,0:T(8,128)S(1)} %bitcast.31, ...), custom_call_target="tpu_custom_call" | custom-call | flops 2621440 | bytes 2621440 | tf_op jit(solution)/shard_map/transport_outer_rows/pallas_call | solution.py:468
  69.1 0.1 collective-permute-start.11
  69.2 2.5 %collective-permute-done.12.rest_1_ = f32[16,128,128]{2,1,0:T(8,128)S(1)} collective-permute-done((f32[16,128,128]{2,1,0:T(8,128)S(1)}, f32[16,128,128]{2,1,0:T(8,128)S(1)}, u32[]{:S(2)}, u32[]{:S(2)}) %collective-permute-start.12) | collective-permute-done | bytes 1048608 | tf_op jit(solution)/shard_map/ppermute | solution.py:527
  71.7 1.7 %collective-permute-start.16 = (f32[16,32,128]{2,1,0:T(8,128)S(1)}, f32[16,32,128]{2,1,0:T(8,128)S(1)}, u32[]{:S(2)}, u32[]{:S(2)}) collective-permute-start(f32[16,32,128]{2,1,0:T(8,128)S(1)} %get-tuple-element.100), channel_id=1, source_target_pairs={{0,24},{8,16},{16,8},{24,0},{1,25},{9,17},{17,9},{25,1},{2,26},{10... | collective-permute-start | bytes 786440 | tf_op jit(solution)/shard_map/ppermute | solution.py:413
  73.3 0.1 pad_maximum_fusion.refs_2_
  73.4 0.1 pad_maximum_fusion.1.refs_16_
  73.5 3.5 %couple_sections.4 = (f32[64,160,128]{2,1,0:T(8,128)}, f32[5,8,512]{2,1,0:T(8,128)}, f32[8,64,512]{2,1,0:T(8,128)S(1)}) custom-call(s32[2]{0:T(128)S(1)} %pad_add_fusion.place_ref.refs_0_, f32[64]{0:T(128)S(1)} %copy-done.4, bf16[64,192]{1,0:T(8,128)(2,1)S(1)} %pad_maximum_fusion.refs_2_, f32[32,128]{1,0:T(8,128)S(1)} %bitcast.23, ...), custom_call_target="tpu_custom_call" | custom-call | flops 33554432 | bytes 3145728 | tf_op jit(solution)/shard_map/couple_sections/pallas_call | solution.py:567
  77.0 1.2 %collective-permute-done.11.refs_14_ = f32[16,32,128]{2,1,0:T(8,128)S(1)} collective-permute-done((f32[16,32,128]{2,1,0:T(8,128)S(1)}, f32[16,32,128]{2,1,0:T(8,128)S(1)}, u32[]{:S(2)}, u32[]{:S(2)}) %collective-permute-start.11) | collective-permute-done | bytes 262176 | tf_op jit(solution)/shard_map/ppermute | solution.py:413
  78.3 2.3 %transport_outer_rows.6 = (f32[16,16,128]{2,1,0:T(8,128)S(1)}, f32[16,16,128]{2,1,0:T(8,128)S(1)}, f32[16,16,128]{2,1,0:T(8,128)S(1)}, f32[16,16,128]{2,1,0:T(8,128)S(1)}) custom-call(s32[2]{0:T(128)S(1)} %pad_add_fusion.place_ref.refs_0_, f32[16]{0:T(128)S(1)} %copy-done.2, f32[16]{0:T(128)S(1)} %copy-done.3, f32[5,16]{1,0:T(8,128)S(1)} %bitcast.32, ...), custom_call_target="tpu_custom_call" | custom-call | flops 1310720 | bytes 1310720 | tf_op jit(solution)/shard_map/transport_outer_rows/pallas_call | solution.py:468
  80.6 0.1 collective-permute-start.14
  80.6 0.2 collective-permute-start.19
  80.8 1.7 %collective-permute-start.20 = (f32[16,16,128]{2,1,0:T(8,128)S(1)}, f32[16,16,128]{2,1,0:T(8,128)S(1)}, u32[]{:S(2)}, u32[]{:S(2)}) collective-permute-start(f32[16,16,128]{2,1,0:T(8,128)S(1)} %get-tuple-element.105), channel_id=1, source_target_pairs={{0,24},{8,16},{16,8},{24,0},{1,25},{9,17},{17,9},{25,1},{2,26},{10... | collective-permute-start | bytes 393224 | tf_op jit(solution)/shard_map/ppermute | solution.py:413
  82.5 2.3 %transport_outer_rows.7 = (f32[16,16,128]{2,1,0:T(8,128)S(1)}, f32[16,16,128]{2,1,0:T(8,128)S(1)}, f32[16,16,128]{2,1,0:T(8,128)S(1)}, f32[16,16,128]{2,1,0:T(8,128)S(1)}) custom-call(s32[2]{0:T(128)S(1)} %pad_add_fusion.place_ref.refs_0_, f32[16]{0:T(128)S(1)} %copy-done.2, f32[16]{0:T(128)S(1)} %copy-done.3, f32[5,16]{1,0:T(8,128)S(1)} %bitcast.33, ...), custom_call_target="tpu_custom_call" | custom-call | flops 1310720 | bytes 1310720 | tf_op jit(solution)/shard_map/transport_outer_rows/pallas_call | solution.py:468
  84.8 0.4 collective-permute-start.17
  85.2 1.4 %collective-permute-start.18 = (f32[16,16,128]{2,1,0:T(8,128)S(1)}, f32[16,16,128]{2,1,0:T(8,128)S(1)}, u32[]{:S(2)}, u32[]{:S(2)}) collective-permute-start(f32[16,16,128]{2,1,0:T(8,128)S(1)} %get-tuple-element.103), channel_id=1, source_target_pairs={{0,24},{8,16},{16,8},{24,0},{1,25},{9,17},{17,9},{25,1},{2,26},{10... | collective-permute-start | bytes 393224 | tf_op jit(solution)/shard_map/ppermute | solution.py:413
  86.6 0.4 collective-permute-start.15
  87.0 4.8 %couple_sections.5 = (f32[64,160,128]{2,1,0:T(8,128)}, f32[5,8,512]{2,1,0:T(8,128)}) custom-call(s32[2]{0:T(128)S(1)} %pad_add_fusion.place_ref.refs_0_, f32[64]{0:T(128)S(1)} %copy-done.4, bf16[64,192]{1,0:T(8,128)(2,1)S(1)} %pad_maximum_fusion.refs_2_, f32[32,128]{1,0:T(8,128)S(1)} %bitcast.24, ...), custom_call_target="tpu_custom_call", output_to_operand_aliasing={{0}: (17, {}), {1}: (18, {})} | custom-call | flops 67108864 | bytes 6291456 | tf_op jit(solution)/shard_map/couple_sections/pallas_call | solution.py:567
  91.8 3.1 %couple_sections.6 = (f32[64,160,128]{2,1,0:T(8,128)}, f32[5,8,512]{2,1,0:T(8,128)}) custom-call(s32[2]{0:T(128)S(1)} %pad_add_fusion.place_ref.refs_0_, f32[64]{0:T(128)S(1)} %copy-done.4, bf16[64,192]{1,0:T(8,128)(2,1)S(1)} %pad_maximum_fusion.refs_2_, f32[32,128]{1,0:T(8,128)S(1)} %bitcast.25, ...), custom_call_target="tpu_custom_call", output_to_operand_aliasing={{0}: (17, {}), {1}: (18, {})} | custom-call | flops 33554432 | bytes 3145728 | tf_op jit(solution)/shard_map/couple_sections/pallas_call | solution.py:567
  94.9 3.1 %couple_sections.7 = (f32[64,160,128]{2,1,0:T(8,128)}, f32[5,8,512]{2,1,0:T(8,128)}) custom-call(s32[2]{0:T(128)S(1)} %pad_add_fusion.place_ref.refs_0_, f32[64]{0:T(128)S(1)} %copy-done.4, bf16[64,192]{1,0:T(8,128)(2,1)S(1)} %pad_maximum_fusion.refs_2_, f32[32,128]{1,0:T(8,128)S(1)} %bitcast.26, ...), custom_call_target="tpu_custom_call", output_to_operand_aliasing={{0}: (17, {}), {1}: (18, {})} | custom-call | flops 33554432 | bytes 3145728 | tf_op jit(solution)/shard_map/couple_sections/pallas_call | solution.py:567
  (30 shorter events, 0.1 us)
Async XLA Ops:
  1.6 0.7 copy-start.1
  2.3 8.8 %copy-start.2 = (f32[16]{0:T(128)S(1)}, f32[16]{0:T(128)}, u32[]{:S(2)}) copy-start(f32[16]{0:T(128)} %ux_ref.15) | copy-start | bytes 196
  4.4 11.9 %copy-start = (f32[16,5]{0,1:T(8,128)S(1)}, f32[16,5]{0,1:T(8,128)}, u32[]{:S(2)}) copy-start(f32[16,5]{0,1:T(8,128)} %param.13) | copy-start | bytes 964
  4.5 11.9 %copy-start.3 = (f32[16]{0:T(128)S(1)}, f32[16]{0:T(128)}, u32[]{:S(2)}) copy-start(f32[16]{0:T(128)} %uy_ref.13) | copy-start | bytes 196
  4.5 19.1 %collective-permute-start = (f32[18,64,128]{2,1,0:T(8,128)S(1)}, f32[18,64,128]{2,1,0:T(8,128)S(1)}, u32[]{:S(2)}, u32[]{:S(2)}) collective-permute-start(f32[18,64,128]{2,1,0:T(8,128)S(1)} %get-tuple-element.68.own_ref), channel_id=1, source_target_pairs={{2,0},{4,2},{6,4},{1,3},{3,5},{5,7},{10,8},{12,10},{14,12},{9,11},... | collective-permute-start | bytes 1769480 | tf_op jit(solution)/shard_map/ppermute | solution.py:530
  5.8 29.3 %collective-permute-start.9 = (f32[16,128,128]{2,1,0:T(8,128)S(1)}, f32[16,128,128]{2,1,0:T(8,128)S(1)}, u32[]{:S(2)}, u32[]{:S(2)}) collective-permute-start(f32[16,128,128]{2,1,0:T(8,128)S(1)} %get-tuple-element.83), channel_id=1, source_target_pairs={{0,1},{1,0},{2,3},{3,2},{4,5},{5,4},{6,7},{7,6},{8,9},{9,8},{10,11... | collective-permute-start | bytes 3145736 | tf_op jit(solution)/shard_map/ppermute | solution.py:527
  15.0 31.5 %collective-permute-start.2 = (f32[16,128,128]{2,1,0:T(8,128)S(1)}, f32[16,128,128]{2,1,0:T(8,128)S(1)}, u32[]{:S(2)}, u32[]{:S(2)}) collective-permute-start(f32[16,128,128]{2,1,0:T(8,128)S(1)} %get-tuple-element.61._.own_ref), channel_id=1, source_target_pairs={{2,0},{4,2},{6,4},{1,3},{3,5},{5,7},{10,8},{12,10},{14,12},{9,11},... | collective-permute-start | bytes 3145736 | tf_op jit(solution)/shard_map/ppermute | solution.py:530
  22.7 36.6 %copy-start.5 = (f32[64,64]{1,0:T(8,128)S(1)}, f32[64,64]{1,0:T(8,128)}, u32[]{:S(2)}) copy-start(f32[64,64]{1,0:T(8,128)} %param.17) | copy-start | bytes 49156
  24.5 22.0 %collective-permute-start.1 = (f32[18,64,128]{2,1,0:T(8,128)S(1)}, f32[18,64,128]{2,1,0:T(8,128)S(1)}, u32[]{:S(2)}, u32[]{:S(2)}) collective-permute-start(f32[18,64,128]{2,1,0:T(8,128)S(1)} %relay_upwind_rows.2._), channel_id=1, source_target_pairs={{0,1},{1,0},{2,3},{3,2},{4,5},{5,4},{6,7},{7,6},{8,9},{9,8},{10,11... | collective-permute-start | bytes 1769480 | tf_op jit(solution)/shard_map/ppermute | solution.py:527
  26.0 23.4 %collective-permute-start.3 = (f32[16,80,128]{2,1,0:T(8,128)S(1)}, f32[16,80,128]{2,1,0:T(8,128)S(1)}, u32[]{:S(2)}, u32[]{:S(2)}) collective-permute-start(f32[16,80,128]{2,1,0:T(8,128)S(1)} %get-tuple-element.70), channel_id=1, source_target_pairs={{0,24},{8,16},{16,8},{24,0},{1,25},{9,17},{17,9},{25,1},{2,26},{10... | collective-permute-start | bytes 1966088 | tf_op jit(solution)/shard_map/ppermute | solution.py:413
  26.1 31.0 %collective-permute-start.4 = (f32[16,80,128]{2,1,0:T(8,128)S(1)}, f32[16,80,128]{2,1,0:T(8,128)S(1)}, u32[]{:S(2)}, u32[]{:S(2)}) collective-permute-start(f32[16,80,128]{2,1,0:T(8,128)S(1)} %get-tuple-element.75), channel_id=1, source_target_pairs={{0,16},{8,24},{16,0},{24,8},{1,17},{9,25},{17,1},{25,9},{2,18},{10... | collective-permute-start | bytes 1966088 | tf_op jit(solution)/shard_map/ppermute | solution.py:413
  35.0 30.6 %collective-permute-start.10 = (f32[16,128,128]{2,1,0:T(8,128)S(1)}, f32[16,128,128]{2,1,0:T(8,128)S(1)}, u32[]{:S(2)}, u32[]{:S(2)}) collective-permute-start(f32[16,128,128]{2,1,0:T(8,128)S(1)} %collective-permute-done.9.rest_2_.rest_4_), channel_id=1, source_target_pairs={{0,2},{2,4},{4,6},{3,1},{5,3},{7,5},{8,10},{10,12},{12,14},{11,9},... | collective-permute-start | bytes 3145736 | tf_op jit(solution)/shard_map/ppermute | solution.py:530
  47.5 24.1 %copy-start.6 = (f32[64,64]{1,0:T(8,128)S(1)}, f32[64,64]{1,0:T(8,128)}, u32[]{:S(2)}) copy-start(f32[64,64]{1,0:T(8,128)} %param.16) | copy-start | bytes 49156
  47.5 25.9 %copy-start.7 = (f32[8,512]{1,0:T(8,128)S(1)}, f32[8,512]{1,0:T(8,128)}, u32[]{:S(2)}) copy-start(f32[8,512]{1,0:T(8,128)} %param.19) | copy-start | bytes 49156
  47.5 26.0 %copy-start.4 = (f32[64]{0:T(128)S(1)}, f32[64]{0:T(128)}, u32[]{:S(2)}) copy-start(f32[64]{0:T(128)} %refs_1_.7) | copy-start | bytes 772
  47.5 24.1 %collective-permute-start.12 = (f32[16,128,128]{2,1,0:T(8,128)S(1)}, f32[16,128,128]{2,1,0:T(8,128)S(1)}, u32[]{:S(2)}, u32[]{:S(2)}) collective-permute-start(f32[16,128,128]{2,1,0:T(8,128)S(1)} %relay_upwind_rows.3._), channel_id=1, source_target_pairs={{0,1},{1,0},{2,3},{3,2},{4,5},{5,4},{6,7},{7,6},{8,9},{9,8},{10,11... | collective-permute-start | bytes 3145736 | tf_op jit(solution)/shard_map/ppermute | solution.py:527
  57.0 2.1 %collective-permute-start.5 = (f32[16,80,128]{2,1,0:T(8,128)S(1)}, f32[16,80,128]{2,1,0:T(8,128)S(1)}, u32[]{:S(2)}, u32[]{:S(2)}) collective-permute-start(f32[16,80,128]{2,1,0:T(8,128)S(1)} %get-tuple-element.76), channel_id=1, source_target_pairs={{0,8},{8,0},{16,24},{24,16},{1,9},{9,1},{17,25},{25,17},{2,10},{10... | collective-permute-start | bytes 1966088 | tf_op jit(solution)/shard_map/ppermute | solution.py:413
  57.1 6.5 %collective-permute-start.7 = (f32[17,16,128]{2,1,0:T(8,128)S(1)}, f32[17,16,128]{2,1,0:T(8,128)S(1)}, u32[]{:S(2)}, u32[]{:S(2)}) collective-permute-start(f32[17,16,128]{2,1,0:T(8,128)S(1)} %get-tuple-element.79), channel_id=1, source_target_pairs={{0,16},{8,24},{16,0},{24,8},{1,17},{9,25},{17,1},{25,9},{2,18},{10... | collective-permute-start | bytes 417800 | tf_op jit(solution)/shard_map/ppermute | solution.py:413
  57.8 7.8 %collective-permute-start.8 = (f32[17,16,128]{2,1,0:T(8,128)S(1)}, f32[17,16,128]{2,1,0:T(8,128)S(1)}, u32[]{:S(2)}, u32[]{:S(2)}) collective-permute-start(f32[17,16,128]{2,1,0:T(8,128)S(1)} %get-tuple-element.81), channel_id=1, source_target_pairs={{0,24},{8,16},{16,8},{24,0},{1,25},{9,17},{17,9},{25,1},{2,26},{10... | collective-permute-start | bytes 417800 | tf_op jit(solution)/shard_map/ppermute | solution.py:413
  59.1 10.0 %collective-permute-start.6 = (f32[17,16,128]{2,1,0:T(8,128)S(1)}, f32[17,16,128]{2,1,0:T(8,128)S(1)}, u32[]{:S(2)}, u32[]{:S(2)}) collective-permute-start(f32[17,16,128]{2,1,0:T(8,128)S(1)} %get-tuple-element.77), channel_id=1, source_target_pairs={{0,8},{8,0},{16,24},{24,16},{1,9},{9,1},{17,25},{25,17},{2,10},{10... | collective-permute-start | bytes 417800 | tf_op jit(solution)/shard_map/ppermute | solution.py:413
  69.1 9.2 %collective-permute-start.11 = (f32[16,32,128]{2,1,0:T(8,128)S(1)}, f32[16,32,128]{2,1,0:T(8,128)S(1)}, u32[]{:S(2)}, u32[]{:S(2)}) collective-permute-start(f32[16,32,128]{2,1,0:T(8,128)S(1)} %get-tuple-element.88), channel_id=1, source_target_pairs={{0,16},{8,24},{16,0},{24,8},{1,17},{9,25},{17,1},{25,9},{2,18},{10... | collective-permute-start | bytes 786440 | tf_op jit(solution)/shard_map/ppermute | solution.py:413
  71.6 8.9 %collective-permute-start.13 = (f32[16,32,128]{2,1,0:T(8,128)S(1)}, f32[16,32,128]{2,1,0:T(8,128)S(1)}, u32[]{:S(2)}, u32[]{:S(2)}) collective-permute-start(f32[16,32,128]{2,1,0:T(8,128)S(1)} %get-tuple-element.95), channel_id=1, source_target_pairs={{0,8},{8,0},{16,24},{24,16},{1,9},{9,1},{17,25},{25,17},{2,10},{10... | collective-permute-start | bytes 786440 | tf_op jit(solution)/shard_map/ppermute | solution.py:413
  71.7 13.1 %collective-permute-start.16 = (f32[16,32,128]{2,1,0:T(8,128)S(1)}, f32[16,32,128]{2,1,0:T(8,128)S(1)}, u32[]{:S(2)}, u32[]{:S(2)}) collective-permute-start(f32[16,32,128]{2,1,0:T(8,128)S(1)} %get-tuple-element.100), channel_id=1, source_target_pairs={{0,24},{8,16},{16,8},{24,0},{1,25},{9,17},{17,9},{25,1},{2,26},{10... | collective-permute-start | bytes 786440 | tf_op jit(solution)/shard_map/ppermute | solution.py:413
  80.6 6.0 %collective-permute-start.14 = (f32[16,16,128]{2,1,0:T(8,128)S(1)}, f32[16,16,128]{2,1,0:T(8,128)S(1)}, u32[]{:S(2)}, u32[]{:S(2)}) collective-permute-start(f32[16,16,128]{2,1,0:T(8,128)S(1)} %get-tuple-element.96), channel_id=1, source_target_pairs={{0,8},{8,0},{16,24},{24,16},{1,9},{9,1},{17,25},{25,17},{2,10},{10... | collective-permute-start | bytes 393224 | tf_op jit(solution)/shard_map/ppermute | solution.py:413
  80.6 11.2 %collective-permute-start.19 = (f32[16,16,128]{2,1,0:T(8,128)S(1)}, f32[16,16,128]{2,1,0:T(8,128)S(1)}, u32[]{:S(2)}, u32[]{:S(2)}) collective-permute-start(f32[16,16,128]{2,1,0:T(8,128)S(1)} %get-tuple-element.104), channel_id=1, source_target_pairs={{0,16},{8,24},{16,0},{24,8},{1,17},{9,25},{17,1},{25,9},{2,18},{10... | collective-permute-start | bytes 393224 | tf_op jit(solution)/shard_map/ppermute | solution.py:413
  80.8 11.0 %collective-permute-start.20 = (f32[16,16,128]{2,1,0:T(8,128)S(1)}, f32[16,16,128]{2,1,0:T(8,128)S(1)}, u32[]{:S(2)}, u32[]{:S(2)}) collective-permute-start(f32[16,16,128]{2,1,0:T(8,128)S(1)} %get-tuple-element.105), channel_id=1, source_target_pairs={{0,24},{8,16},{16,8},{24,0},{1,25},{9,17},{17,9},{25,1},{2,26},{10... | collective-permute-start | bytes 393224 | tf_op jit(solution)/shard_map/ppermute | solution.py:413
  84.8 10.1 %collective-permute-start.17 = (f32[16,16,128]{2,1,0:T(8,128)S(1)}, f32[16,16,128]{2,1,0:T(8,128)S(1)}, u32[]{:S(2)}, u32[]{:S(2)}) collective-permute-start(f32[16,16,128]{2,1,0:T(8,128)S(1)} %get-tuple-element.101), channel_id=1, source_target_pairs={{0,16},{8,24},{16,0},{24,8},{1,17},{9,25},{17,1},{25,9},{2,18},{10... | collective-permute-start | bytes 393224 | tf_op jit(solution)/shard_map/ppermute | solution.py:413
  85.2 9.7 %collective-permute-start.18 = (f32[16,16,128]{2,1,0:T(8,128)S(1)}, f32[16,16,128]{2,1,0:T(8,128)S(1)}, u32[]{:S(2)}, u32[]{:S(2)}) collective-permute-start(f32[16,16,128]{2,1,0:T(8,128)S(1)} %get-tuple-element.103), channel_id=1, source_target_pairs={{0,24},{8,16},{16,8},{24,0},{1,25},{9,17},{17,9},{25,1},{2,26},{10... | collective-permute-start | bytes 393224 | tf_op jit(solution)/shard_map/ppermute | solution.py:413
  86.6 8.3 %collective-permute-start.15 = (f32[16,16,128]{2,1,0:T(8,128)S(1)}, f32[16,16,128]{2,1,0:T(8,128)S(1)}, u32[]{:S(2)}, u32[]{:S(2)}) collective-permute-start(f32[16,16,128]{2,1,0:T(8,128)S(1)} %get-tuple-element.97), channel_id=1, source_target_pairs={{0,8},{8,0},{16,24},{24,16},{1,9},{9,1},{17,25},{25,17},{2,10},{10... | collective-permute-start | bytes 393224 | tf_op jit(solution)/shard_map/ppermute | solution.py:413
